TPU v7x, 32 devices: a whole 2x2x4 slice. The times are simulated.
32 devices in a mesh: dp: 4 (over z), seq: 8 (over y, x, core).
Axes of the slice: x: 2, y: 2, z: 4, core: 2. Of those that a mesh axis runs over, the one named last changes fastest.
Arguments:
- x_rows: bfloat16 [4, 1024, 1024], P('dp', 'seq'), may hold values from -6 to 6
- lengths: int32 [4, 8], P('dp'), may hold values from 1 to 512, 1024 in all within a row
- targets: int32 [4, 8], P('dp'), may hold values from 1 to 64
- w_in: bfloat16 [1024, 2048], replicated, may hold values from -0.1875 to 0.1875
- w_out: bfloat16 [512, 1024], replicated, may hold values from -0.25 to 0.25
- w_score: bfloat16 [1024, 256], replicated, may hold values from -0.1875 to 0.1875
- head_score: float32 [256], replicated, may hold values from -0.375 to 0.375
- grad_out: bfloat16 [4, 1024, 1024], P('dp', 'seq'), may hold values from -6 to 6
- grad_score: float32 [4, 1024], P('dp', 'seq'), may hold values from -6 to 6
Outputs:
- d_x: bfloat16 [4, 1024, 1024], P('dp', 'seq')
- d_w_in: float32 [1024, 2048], P('seq', 'dp')
- d_w_out: float32 [512, 1024], P('seq', 'dp')
- d_w_score: float32 [1024, 256], P('seq', 'dp')
- d_head: float32 [256], replicated
Inputs may be any that keep to these rules, and one draw needn't show every extreme that they name: Each row lists the lengths of 8 histories packed end to end in the 1024 positions of a group; they sum to 1024 and the largest is 512.
All inputs are finite; a program needn't handle non-finite values.
Results may differ from a plain program's by a relative error of at most 0.0084.
Values may be sent and summed in bfloat16 or wider, within the bound.
A program may use at most 64 MiB of HBM per device.

v0:
```python
import math

import jax
import jax.numpy as jnp
from jax import lax
from jax.sharding import PartitionSpec as P

HEADS = 4
DH = 128


NORM_EPS = 1e-05


def shifted(x, axis, by):
    length = lax.axis_size(axis)
    pairs = [(i, i + by) for i in range(length) if 0 <= i + by < length]
    return lax.ppermute(x, axis, pairs)


def silu_slope(value):
    sigma = jax.nn.sigmoid(value)
    return sigma * (1.0 + value * (1.0 - sigma))


def norm_rows(value):
    centre = value - jnp.mean(value, axis=-1, keepdims=True)
    inverse = lax.rsqrt(jnp.mean(centre * centre, axis=-1, keepdims=True) + NORM_EPS)
    return (centre * inverse, inverse)


def norm_back(grad, normed, inverse):
    return inverse * (
        grad
        - jnp.mean(grad, axis=-1, keepdims=True)
        - normed * jnp.mean(grad * normed, axis=-1, keepdims=True)
    )


def row_marks(positions, lengths, targets):
    ends = jnp.cumsum(lengths)
    starts = ends - lengths
    counts = jnp.minimum(targets, lengths - 1)
    inside = (positions[:, None] >= starts[None, :]) & (positions[:, None] < ends[None, :])
    segment = jnp.sum((positions[:, None] >= ends[None, :]).astype(jnp.int32), axis=1)
    first_target = jnp.sum(jnp.where(inside, (ends - counts)[None, :], 0), axis=1)
    return (segment, positions >= first_target)


def visible(query_pos, query_seg, key_pos, key_seg, key_tgt):
    same_hist = query_seg[:, None] == key_seg[None, :]
    causal = key_pos[None, :] <= query_pos[:, None]
    open_key = jnp.logical_not(key_tgt)[None, :] | (key_pos[None, :] == query_pos[:, None])
    return (same_hist & causal & open_key)[None, :, :]


def weights_of(query_b, key_b, mask, divisor):
    raw_scores = jnp.einsum(
        "rhd,chd->hrc", query_b, key_b, preferred_element_type=jnp.float32
    ) * DH ** (-0.5)
    attn_b = jnp.where(mask, jax.nn.silu(raw_scores) / divisor, 0.0).astype(jnp.bfloat16)
    return (raw_scores, attn_b)


def score_grads(raw_scores, mask, grad_b, value_b, divisor):
    grad_attn = jnp.einsum("rhd,chd->hrc", grad_b, value_b, preferred_element_type=jnp.float32)
    factor = jnp.where(mask, silu_slope(raw_scores) * DH ** (-0.5) / divisor, 0.0)
    return (grad_attn * factor).astype(jnp.bfloat16)


def on_device(x_rows, lengths, targets, w_in, w_out, w_score, head_score, grad_out, grad_score):
    rows = x_rows.shape[1]
    seq_count = lax.axis_size("seq")
    total = rows * seq_count
    width = w_out.shape[0]
    divisor = float(total // 2)
    hist_len = lengths[0]
    hist_tgt = targets[0]
    own_start = lax.axis_index("seq") * rows
    positions = own_start + jnp.arange(rows, dtype=jnp.int32)
    all_pos = jnp.arange(total, dtype=jnp.int32)
    segment, target = row_marks(positions, hist_len, hist_tgt)
    all_seg, all_tgt = row_marks(all_pos, hist_len, hist_tgt)
    x_float = x_rows[0].astype(jnp.float32)
    normed, inverse = norm_rows(x_float)
    normed_b = normed.astype(jnp.bfloat16)
    pre_act = jnp.dot(normed_b, w_in, preferred_element_type=jnp.float32)
    hidden_b = jax.nn.silu(pre_act).astype(jnp.bfloat16)
    gate_b = hidden_b[:, 0:width]
    value_b = hidden_b[:, width : 2 * width].reshape(rows, HEADS, DH)
    query_b = hidden_b[:, 2 * width : 3 * width].reshape(rows, HEADS, DH)
    key_b = hidden_b[:, 3 * width : 4 * width].reshape(rows, HEADS, DH)
    key_all, value_all = (
        lax.all_gather(key_b, "seq", axis=0, tiled=True),
        lax.all_gather(value_b, "seq", axis=0, tiled=True),
    )
    block_rows = math.gcd(512, total)
    block_count = total // block_rows

    def key_slice(array, number):
        return lax.dynamic_slice_in_dim(array, number * block_rows, block_rows, 0)

    def block_mask(number):
        return visible(
            positions,
            segment,
            key_slice(all_pos, number),
            key_slice(all_seg, number),
            key_slice(all_tgt, number),
        )

    def forward_step(carry, number):
        raw_scores, attn_b = weights_of(
            query_b, key_slice(key_all, number), block_mask(number), divisor
        )
        return (
            carry
            + jnp.einsum(
                "hrc,chd->rhd",
                attn_b,
                key_slice(value_all, number),
                preferred_element_type=jnp.float32,
            ),
            None,
        )

    numbers = jnp.arange(block_count, dtype=jnp.int32)
    attended, unused = lax.scan(forward_step, jnp.zeros((rows, HEADS, DH), jnp.float32), numbers)
    attended = attended.reshape(rows, width)
    onorm, att_inverse = norm_rows(attended)
    gate_f = gate_b.astype(jnp.float32)
    gated_b = (onorm * gate_f).astype(jnp.bfloat16)
    output = x_float + jnp.dot(gated_b, w_out, preferred_element_type=jnp.float32)
    out_b = output.astype(jnp.bfloat16)
    mid_act = jnp.dot(out_b, w_score, preferred_element_type=jnp.float32)
    weight_c = grad_score[0] * target.astype(jnp.float32)
    head_part = jnp.sum(weight_c[:, None] * jax.nn.silu(mid_act), axis=0)
    d_mid_b = (weight_c[:, None] * head_score[None, :] * silu_slope(mid_act)).astype(jnp.bfloat16)
    score_part = jnp.dot(out_b.T, d_mid_b, preferred_element_type=jnp.float32)
    d_total = grad_out[0].astype(jnp.float32) + jnp.dot(
        d_mid_b, w_score.T, preferred_element_type=jnp.float32
    )
    d_total_b = d_total.astype(jnp.bfloat16)
    out_part = jnp.dot(gated_b.T, d_total_b, preferred_element_type=jnp.float32)
    d_gated = jnp.dot(d_total_b, w_out.T, preferred_element_type=jnp.float32)
    d_gate = d_gated * onorm
    d_att_b = (
        norm_back(d_gated * gate_f, onorm, att_inverse)
        .astype(jnp.bfloat16)
        .reshape(rows, HEADS, DH)
    )

    def query_step(carry, number):
        mask = block_mask(number)
        raw_scores, attn_b = weights_of(query_b, key_slice(key_all, number), mask, divisor)
        d_raw_b = score_grads(raw_scores, mask, d_att_b, key_slice(value_all, number), divisor)
        return (
            carry
            + jnp.einsum(
                "hrc,chd->rhd",
                d_raw_b,
                key_slice(key_all, number),
                preferred_element_type=jnp.float32,
            ),
            None,
        )

    d_query, unused = lax.scan(query_step, jnp.zeros((rows, HEADS, DH), jnp.float32), numbers)

    def key_terms(carry, query_piece, grad_piece, start):
        piece_pos = start + jnp.arange(query_piece.shape[0], dtype=jnp.int32)
        piece_seg, piece_tgt = row_marks(piece_pos, hist_len, hist_tgt)
        mask = visible(piece_pos, piece_seg, positions, segment, target)
        raw_scores, attn_b = weights_of(query_piece, key_b, mask, divisor)
        d_raw_b = score_grads(raw_scores, mask, grad_piece, value_b, divisor)
        d_key = carry[0] + jnp.einsum(
            "hrc,rhd->chd", d_raw_b, query_piece, preferred_element_type=jnp.float32
        )
        d_value = carry[1] + jnp.einsum(
            "hrc,rhd->chd", attn_b, grad_piece, preferred_element_type=jnp.float32
        )
        return (d_key, d_value)

    empty = jnp.zeros((rows, HEADS, DH), jnp.float32)
    own_terms = key_terms((empty, empty), query_b, d_att_b, own_start)

    def later_pairs(step, state):
        moving = shifted(state[0], "seq", -1)
        start = own_start + step * rows
        return (moving, key_terms(state[1], moving[0], moving[1], start))

    final_state = lax.fori_loop(
        1, seq_count, later_pairs, (jnp.stack([query_b, d_att_b]), own_terms)
    )
    d_key, d_value = final_state[1]
    d_hidden = jnp.concatenate(
        [
            d_gate,
            d_value.reshape(rows, width),
            d_query.reshape(rows, width),
            d_key.reshape(rows, width),
        ],
        axis=1,
    )
    d_pre_b = (d_hidden * silu_slope(pre_act)).astype(jnp.bfloat16)
    in_part = jnp.dot(normed_b.T, d_pre_b, preferred_element_type=jnp.float32)
    d_normed = jnp.dot(d_pre_b, w_in.T, preferred_element_type=jnp.float32)
    d_x = (d_total + norm_back(d_normed, normed, inverse)).astype(jnp.bfloat16)
    partial_sums = (
        lax.psum_scatter(in_part, "seq", scatter_dimension=0, tiled=True),
        lax.psum_scatter(out_part, "seq", scatter_dimension=0, tiled=True),
        lax.psum_scatter(score_part, "seq", scatter_dimension=0, tiled=True),
    )
    d_w_in, d_w_out, d_w_score = (
        lax.psum_scatter(partial_sums[0], "dp", scatter_dimension=1, tiled=True),
        lax.psum_scatter(partial_sums[1], "dp", scatter_dimension=1, tiled=True),
        lax.psum_scatter(partial_sums[2], "dp", scatter_dimension=1, tiled=True),
    )
    d_head = lax.psum(head_part, ("dp", "seq"))
    return (d_x[None], d_w_in, d_w_out, d_w_score, d_head)


def solution(mesh):
    placed = (
        P("dp", "seq", None),
        P("dp", None),
        P("dp", None),
        P(),
        P(),
        P(),
        P(),
        P("dp", "seq", None),
        P("dp", "seq"),
    )
    return jax.shard_map(
        on_device,
        mesh=mesh,
        in_specs=placed,
        out_specs=(P("dp", "seq", None), P("seq", "dp"), P("seq", "dp"), P("seq", "dp"), P()),
        check_vma=False,
    )
```

profile of v0, /device:TPU:0, one launch (start us, length us, event | category | flops | bytes accessed | tf_op | source)
XLA Modules:
  0.0 352.0 jit_solution(10664912514754991430)
XLA Ops:
  7.2 1.1 convert_reduce_fusion.1
  8.4 1.2 fusion.88
  9.6 4.1 %multiply_convert_fusion = (bf16[128,2048]{1,0:T(8,128)(2,1)S(1)}, f32[128,2048]{1,0:T(8,128)}) fusion(bf16[1024,2048]{1,0:T(8,128)(2,1)} %param.18, bf16[1,128,1024]{2,1,0:T(8,128)(2,1)} %param.15, f32[128]{0:T(128)S(1)} %add_rsqrt_fusion.1, f32[128]{0:T(128)S(1)} %broadcast_multiply_fusion.5), kind=kOutput, calls=%fused_computation.103 | convolution fusion | flops 538705920 | bytes 6030336 | tf_op jit(solution)/shard_map/dot_general | solution.py:87
  18.3 1.4 or_and_fusion.3
  19.7 0.9 convolution_multiply_fusion.4
  21.3 19.6 %all-gather.3.cloned.1.call-done = bf16[1024,4,128]{2,1,0:T(4,128)(2,1)} async-done(((bf16[128,4,128]{2,1,0:T(4,128)(2,1)}), bf16[1024,4,128]{2,1,0:T(4,128)(2,1)}) %all-gather.3.cloned.1.call-update) | async-done | bytes 1048592 | tf_op jit(solution)/shard_map/all_gather | solution.py:95
  40.9 25.4 %all-gather.5.cloned.1.call-done = bf16[1024,4,128]{2,0,1:T(8,128)(2,1)} async-done(((bf16[128,4,128]{2,0,1:T(8,128)(2,1)}), bf16[1024,4,128]{2,0,1:T(8,128)(2,1)}) %all-gather.5.cloned.1.call-update) | async-done | bytes 1048592 | tf_op jit(solution)/shard_map/all_gather | solution.py:94
  66.3 11.0 %while.45 = (s32[]{:T(128)}, f32[128,4,128]{0,2,1:T(8,128)S(1)}, s32[2]{0:T(128)S(1)}, bf16[1024,4,128]{2,1,0:T(4,128)(2,1)}, s32[128]{0:T(128)}, /*index=5*/s32...) while((s32[]{:T(128)}, f32[128,4,128]{0,2,1:T(8,128)S(1)}, ...), condition=%wide.region_8.9_spmd.clone, body=%wide.region_7.8_spmd.clone.sunk | while | flops 136839808 | bytes 2899185 | solution.py:128
  67.8 0.9 or_and_fusion.7
  68.8 1.2 constant_dynamic-slice_fusion.4
  70.0 1.8 fusion.166
  73.3 0.9 or_and_fusion.7
  74.3 1.2 constant_dynamic-slice_fusion.4
  75.5 1.8 fusion.166
  78.8 2.0 multiply_reduce_fusion.2
  80.8 1.3 fusion.124
  82.1 1.4 convolution_add_fusion.1
  83.6 0.8 copy-done.2
  85.0 0.9 fusion.97
  85.8 1.6 copy_bitcast_fusion.3
  87.5 16.4 %while.46 = (s32[]{:T(128)}, f32[128,4,128]{0,2,1:T(8,128)}, s32[2]{0:T(128)S(1)}, bf16[1024,4,128]{2,0,1:T(8,128)(2,1)}, bf16[1024,4,128]{2,1,0:T(4,128)(2,1)S(...) while((s32[]{:T(128)}, f32[128,4,128]{0,2,1:T(8,128)}, ...), condition=%wide.region_18.19_spmd.clone, body=%wide.region_17.18_spmd.clone.sunk | while | flops 204997248 | bytes 5651709 | solution.py:168
  89.0 1.6 or_and_fusion.8
  90.6 1.0 constant_dynamic-slice_fusion.5
  91.5 1.3 fusion.172
  92.9 2.8 fusion.173
  97.1 1.6 or_and_fusion.8
  98.7 1.0 constant_dynamic-slice_fusion.5
  99.7 1.3 fusion.172
  101.0 2.9 fusion.173
  103.9 1.0 stack_reshape.7
  104.9 1.2 convolution_bitcast_fusion.4
  106.3 1.5 convolution_bitcast_fusion.5
  108.9 1.9 fusion.104
  110.8 71.7 %while.47 = (s32[]{:T(128)}, bf16[2,128,4,128]{3,1,2,0:T(8,128)(2,1)}, f32[128,4,128]{2,0,1:T(8,128)S(1)}, f32[128,4,128]{2,0,1:T(8,128)S(1)}, bf16[128,4,128]{2...) while((s32[]{:T(128)}, ...), condition=%wide.region_16.17_spmd.clone.clone, body=%wide.region_14.16_spmd.clone.clone.sunk | while | flops 68586624 | bytes 4247901 | solution.py:192
  110.8 1.4 collective-permute-start
  113.0 0.8 or_and_fusion.9
  113.7 0.9 collective-permute-done
  115.8 1.3 fusion.176
  117.2 1.3 collective-permute-start
  119.9 4.9 %collective-permute-done = bf16[2,128,4,128]{3,1,2,0:T(8,128)(2,1)S(1)} collective-permute-done((bf16[2,128,4,128]{3,1,2,0:T(8,128)(2,1)}, bf16[2,128,4,128]{3,1,2,0:T(8,128)(2,1)S(1)}, u32[]{:S(2)}, u32[]{:S(2)}) %collective-permute-start) | collective-permute-done | bytes 262176 | tf_op jit(solution)/shard_map/while/body/eval_jaxpr/ppermute | solution.py:18
  126.1 1.3 fusion.176
  127.4 1.3 collective-permute-start
  130.2 5.2 %collective-permute-done = bf16[2,128,4,128]{3,1,2,0:T(8,128)(2,1)S(1)} collective-permute-done((bf16[2,128,4,128]{3,1,2,0:T(8,128)(2,1)}, bf16[2,128,4,128]{3,1,2,0:T(8,128)(2,1)S(1)}, u32[]{:S(2)}, u32[]{:S(2)}) %collective-permute-start) | collective-permute-done | bytes 262176 | tf_op jit(solution)/shard_map/while/body/eval_jaxpr/ppermute | solution.py:18
  136.6 1.3 fusion.176
  138.0 1.3 collective-permute-start
  140.0 0.8 or_and_fusion.9
  140.8 5.0 %collective-permute-done = bf16[2,128,4,128]{3,1,2,0:T(8,128)(2,1)S(1)} collective-permute-done((bf16[2,128,4,128]{3,1,2,0:T(8,128)(2,1)}, bf16[2,128,4,128]{3,1,2,0:T(8,128)(2,1)S(1)}, u32[]{:S(2)}, u32[]{:S(2)}) %collective-permute-start) | collective-permute-done | bytes 262176 | tf_op jit(solution)/shard_map/while/body/eval_jaxpr/ppermute | solution.py:18
  147.0 1.3 fusion.176
  148.4 1.3 collective-permute-start
  151.2 6.9 %collective-permute-done = bf16[2,128,4,128]{3,1,2,0:T(8,128)(2,1)S(1)} collective-permute-done((bf16[2,128,4,128]{3,1,2,0:T(8,128)(2,1)}, bf16[2,128,4,128]{3,1,2,0:T(8,128)(2,1)S(1)}, u32[]{:S(2)}, u32[]{:S(2)}) %collective-permute-start) | collective-permute-done | bytes 262176 | tf_op jit(solution)/shard_map/while/body/eval_jaxpr/ppermute | solution.py:18
  159.3 1.3 fusion.176
  160.7 1.3 collective-permute-start
  163.4 5.2 %collective-permute-done = bf16[2,128,4,128]{3,1,2,0:T(8,128)(2,1)S(1)} collective-permute-done((bf16[2,128,4,128]{3,1,2,0:T(8,128)(2,1)}, bf16[2,128,4,128]{3,1,2,0:T(8,128)(2,1)S(1)}, u32[]{:S(2)}, u32[]{:S(2)}) %collective-permute-start) | collective-permute-done | bytes 262176 | tf_op jit(solution)/shard_map/while/body/eval_jaxpr/ppermute | solution.py:18
  169.8 1.3 fusion.176
  171.1 1.3 collective-permute-start
  173.9 6.1 %collective-permute-done = bf16[2,128,4,128]{3,1,2,0:T(8,128)(2,1)S(1)} collective-permute-done((bf16[2,128,4,128]{3,1,2,0:T(8,128)(2,1)}, bf16[2,128,4,128]{3,1,2,0:T(8,128)(2,1)S(1)}, u32[]{:S(2)}, u32[]{:S(2)}) %collective-permute-start) | collective-permute-done | bytes 262176 | tf_op jit(solution)/shard_map/while/body/eval_jaxpr/ppermute | solution.py:18
  181.2 1.3 fusion.176
  182.6 5.9 %fusion.120 = f32[1024,2048]{1,0:T(8,128)} fusion(bf16[1,128,1024]{2,1,0:T(8,128)(2,1)S(1)} %copy-done.4, f32[128]{0:T(128)} %copy-done.15, f32[128]{0:T(128)} %copy-done.13, f32[128,512]{1,0:T(8,128)S(1)} %copy_bitcast_fusion, f32[128,512]{1,0:T(8,128)S(1)} %copy.94, f32[128,512]{1,0:T(8,128)S(1)} %copy_bitcast_fusion.1, f32[128,512]{1,0:T(8,128)S(1)} %copy-done.9, ...), kind=kOutput, calls=%fused_computation.194 | convolution fusion | flops 540540928 | bytes 10748928 | tf_op jit(solution)/shard_map/dot_general | solution.py:206
  188.6 1.7 copy.95
  191.1 83.1 %reduce-scatter.9.cloned.1.call-done = f32[128,2048]{1,0:T(8,128)} async-done(((f32[1024,2048]{1,0:T(8,128)}), f32[128,2048]{1,0:T(8,128)}) %reduce-scatter.9.cloned.1.call-update) | async-done | bytes 1048592 | tf_op jit(solution)/shard_map/reduce_scatter | solution.py:210
  274.2 39.4 %psum.7 = f32[256]{0:T(256)} all-reduce(f32[256]{0:T(256)S(1)} %copy-done.18), channel_id=1, replica_groups=mesh['dp'=4,'seq'=8] {'dp','seq'}, use_global_device_ids=true, to_apply=%region_28.29 | all-reduce | flops 256 | bytes 2048 | tf_op jit(solution)/shard_map/psum | solution.py:219
  313.6 4.1 %fusion.125 = (f32[128]{0:T(128)S(1)}, f32[128]{0:T(128)S(1)}, f32[128,1024]{1,0:T(8,128)S(1)}) fusion(f32[128]{0:T(128)S(1)} %copy-done.16, f32[128]{0:T(128)S(1)} %copy-done.14, bf16[1,128,1024]{2,1,0:T(8,128)(2,1)S(1)} %copy-done.4, bf16[1024,2048]{1,0:T(8,128)(2,1)} %param.18, f32[128,512]{1,0:T(8,128)S(1)} %copy_bitcast_fusion, ...), kind=kOutput, calls=%fused_computation.197 | convolution fusion | flops 540802816 | bytes 7079936 | tf_op jit(solution)/shard_map/dot_general | solution.py:207
  317.7 1.0 fusion.90
  318.7 26.5 %reduce-scatter.11.cloned.1.call-done = f32[128,512]{1,0:T(8,128)} async-done(((f32[128,2048]{1,0:T(8,128)}), f32[128,512]{1,0:T(8,128)}) %reduce-scatter.11.cloned.1.call-update) | async-done | bytes 262160 | tf_op jit(solution)/shard_map/reduce_scatter | solution.py:215
  (166 shorter events, 29.8 us)
Async XLA Ops:
  7.2 71.3 %copy-start = (bf16[512,1024]{1,0:T(8,128)(2,1)S(1)}, bf16[512,1024]{1,0:T(8,128)(2,1)}, u32[]{:S(2)}) copy-start(bf16[512,1024]{1,0:T(8,128)(2,1)} %param.19) | copy-start | bytes 3145732
  7.2 33.7 %all-gather.3.cloned.1.call-start = ((), (), s32[]{:S(2)}) async-start(), calls=%async_computation.6 | async-start | bytes 1179648 | tf_op jit(solution)/shard_map/all_gather | solution.py:95
  8.4 5.3 %copy-start.13 = (f32[128]{0:T(128)}, f32[128]{0:T(128)S(1)}, u32[]{:S(2)}) copy-start(f32[128]{0:T(128)S(1)} %broadcast_multiply_fusion.5) | copy-start | bytes 1540
  9.6 4.1 %copy-start.15 = (f32[128]{0:T(128)}, f32[128]{0:T(128)S(1)}, u32[]{:S(2)}) copy-start(f32[128]{0:T(128)S(1)} %add_rsqrt_fusion.1) | copy-start | bytes 1540
  9.6 5.8 %copy-start.20 = (s32[1,8]{1,0:T(1,128)S(1)}, s32[1,8]{1,0:T(1,128)}, u32[]{:S(2)}) copy-start(s32[1,8]{1,0:T(1,128)} %param.16) | copy-start | bytes 100
  9.6 6.0 %copy-start.19 = (s32[1,8]{1,0:T(1,128)S(1)}, s32[1,8]{1,0:T(1,128)}, u32[]{:S(2)}) copy-start(s32[1,8]{1,0:T(1,128)} %param.17) | copy-start | bytes 100
  9.6 8.7 %copy-start.21 = (f32[1,128]{1,0:T(1,128)S(1)}, f32[1,128]{1,0:T(1,128)}, u32[]{:S(2)}) copy-start(f32[1,128]{1,0:T(1,128)} %param.23) | copy-start | bytes 1540
  13.8 52.5 %copy-start.6 = (bf16[16,4,8,128]{3,2,1,0:T(8,128)(2,1)}, bf16[16,4,8,128]{3,2,1,0:T(8,128)(2,1)S(1)}, u32[]{:S(2)}) copy-start(bf16[16,4,8,128]{3,2,1,0:T(8,128)(2,1)S(1)} %get-tuple-element.807) | copy-start | bytes 393220
  13.8 52.5 %copy-start.11 = (bf16[16,4,8,128]{3,2,1,0:T(8,128)(2,1)}, bf16[16,4,8,128]{3,2,1,0:T(8,128)(2,1)S(1)}, u32[]{:S(2)}) copy-start(bf16[16,4,8,128]{3,2,1,0:T(8,128)(2,1)S(1)} %get-tuple-element.806) | copy-start | bytes 393220
  14.5 51.8 %all-gather.5.cloned.1.call-start = ((), (), s32[]{:S(2)}) async-start(), calls=%async_computation.7 | async-start | bytes 1179648 | tf_op jit(solution)/shard_map/all_gather | solution.py:94
  15.3 173.3 %reduce-scatter.17.cloned.1.call-start = ((), (), s32[]{:S(2)}) async-start(), calls=%async_computation.12 | async-start | bytes 1179648 | tf_op jit(solution)/shard_map/reduce_scatter | solution.py:212
  66.3 12.2 %copy-start.4 = (bf16[1,128,1024]{2,1,0:T(8,128)(2,1)S(1)}, bf16[1,128,1024]{2,1,0:T(8,128)(2,1)}, u32[]{:S(2)}) copy-start(bf16[1,128,1024]{2,1,0:T(8,128)(2,1)} %param.15) | copy-start | bytes 786436
  77.4 3.4 copy-start.17
  77.8 0.7 copy-start.7
  78.8 8.7 %copy-start.1 = (bf16[1024,4,128]{2,1,0:T(4,128)(2,1)S(1)}, bf16[1024,4,128]{2,1,0:T(4,128)(2,1)}, u32[]{:S(2)}) copy-start(bf16[1024,4,128]{2,1,0:T(4,128)(2,1)} %get-tuple-element.1166) | copy-start | bytes 3145732
  83.6 0.8 copy-start.2
  87.4 102.9 %reduce-scatter.13.cloned.1.call-start = ((), (), s32[]{:S(2)}) async-start(), calls=%async_computation.10 | async-start | bytes 2359296 | tf_op jit(solution)/shard_map/reduce_scatter | solution.py:211
  103.9 4.1 %copy-start.12 = (f32[128,4,128]{0,2,1:T(8,128)S(1)}, f32[128,4,128]{0,2,1:T(8,128)}, u32[]{:S(2)}) copy-start(f32[128,4,128]{0,2,1:T(8,128)} %get-tuple-element.482) | copy-start | bytes 786436
  103.9 4.2 %copy-start.10 = (bf16[1,128,4,128]{3,1,2,0:T(8,128)(2,1)S(1)}, bf16[1,128,4,128]{3,1,2,0:T(8,128)(2,1)}, u32[]{:S(2)}) copy-start(bf16[1,128,4,128]{3,1,2,0:T(8,128)(2,1)} %copy.69) | copy-start | bytes 393220
  103.9 5.0 %copy-start.3 = (f32[128,1024]{1,0:T(8,128)S(1)}, f32[128,1024]{1,0:T(8,128)}, u32[]{:S(2)}) copy-start(f32[128,1024]{1,0:T(8,128)} %copy-done.2) | copy-start | bytes 1572868
  103.9 5.0 %copy-start.8 = (bf16[128,512]{1,0:T(8,128)(2,1)S(1)}, bf16[128,512]{1,0:T(8,128)(2,1)}, u32[]{:S(2)}) copy-start(bf16[128,512]{1,0:T(8,128)(2,1)} %copy-done.7) | copy-start | bytes 393220
  106.3 4.5 %copy-start.5 = (bf16[16,4,8,128]{3,2,0,1:T(8,128)(2,1)S(1)}, bf16[16,4,8,128]{3,2,0,1:T(8,128)(2,1)}, u32[]{:S(2)}) copy-start(bf16[16,4,8,128]{3,2,0,1:T(8,128)(2,1)} %copy.124) | copy-start | bytes 393220
  110.8 163.4 %reduce-scatter.9.cloned.1.call-start = ((), (), s32[]{:S(2)}) async-start(), calls=%async_computation.8 | async-start | bytes 9437184 | tf_op jit(solution)/shard_map/reduce_scatter | solution.py:210
  110.8 71.8 %copy-start.9 = (f32[128,512]{1,0:T(8,128)S(1)}, f32[128,512]{1,0:T(8,128)}, u32[]{:S(2)}) copy-start(f32[128,512]{1,0:T(8,128)} %get-tuple-element.804) | copy-start | bytes 786436
  110.8 3.8 %collective-permute-start = (bf16[2,128,4,128]{3,1,2,0:T(8,128)(2,1)}, bf16[2,128,4,128]{3,1,2,0:T(8,128)(2,1)S(1)}, u32[]{:S(2)}, u32[]{:S(2)}) collective-permute-start(bf16[2,128,4,128]{3,1,2,0:T(8,128)(2,1)} %get-tuple-element.1084), channel_id=1, source_target_pairs={{1,0},{2,1},{3,2},{4,3},{5,4},{6,5},{7,6},{9,8},{10,9},{11,10},{12... | collective-permute-start | bytes 786440 | tf_op jit(solution)/shard_map/while/body/eval_jaxpr/ppermute | solution.py:18
  117.2 7.7 %collective-permute-start = (bf16[2,128,4,128]{3,1,2,0:T(8,128)(2,1)}, bf16[2,128,4,128]{3,1,2,0:T(8,128)(2,1)S(1)}, u32[]{:S(2)}, u32[]{:S(2)}) collective-permute-start(bf16[2,128,4,128]{3,1,2,0:T(8,128)(2,1)} %get-tuple-element.1084), channel_id=1, source_target_pairs={{1,0},{2,1},{3,2},{4,3},{5,4},{6,5},{7,6},{9,8},{10,9},{11,10},{12... | collective-permute-start | bytes 786440 | tf_op jit(solution)/shard_map/while/body/eval_jaxpr/ppermute | solution.py:18
  127.4 8.0 %collective-permute-start = (bf16[2,128,4,128]{3,1,2,0:T(8,128)(2,1)}, bf16[2,128,4,128]{3,1,2,0:T(8,128)(2,1)S(1)}, u32[]{:S(2)}, u32[]{:S(2)}) collective-permute-start(bf16[2,128,4,128]{3,1,2,0:T(8,128)(2,1)} %get-tuple-element.1084), channel_id=1, source_target_pairs={{1,0},{2,1},{3,2},{4,3},{5,4},{6,5},{7,6},{9,8},{10,9},{11,10},{12... | collective-permute-start | bytes 786440 | tf_op jit(solution)/shard_map/while/body/eval_jaxpr/ppermute | solution.py:18
  138.0 7.8 %collective-permute-start = (bf16[2,128,4,128]{3,1,2,0:T(8,128)(2,1)}, bf16[2,128,4,128]{3,1,2,0:T(8,128)(2,1)S(1)}, u32[]{:S(2)}, u32[]{:S(2)}) collective-permute-start(bf16[2,128,4,128]{3,1,2,0:T(8,128)(2,1)} %get-tuple-element.1084), channel_id=1, source_target_pairs={{1,0},{2,1},{3,2},{4,3},{5,4},{6,5},{7,6},{9,8},{10,9},{11,10},{12... | collective-permute-start | bytes 786440 | tf_op jit(solution)/shard_map/while/body/eval_jaxpr/ppermute | solution.py:18
  148.4 9.7 %collective-permute-start = (bf16[2,128,4,128]{3,1,2,0:T(8,128)(2,1)}, bf16[2,128,4,128]{3,1,2,0:T(8,128)(2,1)S(1)}, u32[]{:S(2)}, u32[]{:S(2)}) collective-permute-start(bf16[2,128,4,128]{3,1,2,0:T(8,128)(2,1)} %get-tuple-element.1084), channel_id=1, source_target_pairs={{1,0},{2,1},{3,2},{4,3},{5,4},{6,5},{7,6},{9,8},{10,9},{11,10},{12... | collective-permute-start | bytes 786440 | tf_op jit(solution)/shard_map/while/body/eval_jaxpr/ppermute | solution.py:18
  160.7 7.9 %collective-permute-start = (bf16[2,128,4,128]{3,1,2,0:T(8,128)(2,1)}, bf16[2,128,4,128]{3,1,2,0:T(8,128)(2,1)S(1)}, u32[]{:S(2)}, u32[]{:S(2)}) collective-permute-start(bf16[2,128,4,128]{3,1,2,0:T(8,128)(2,1)} %get-tuple-element.1084), channel_id=1, source_target_pairs={{1,0},{2,1},{3,2},{4,3},{5,4},{6,5},{7,6},{9,8},{10,9},{11,10},{12... | collective-permute-start | bytes 786440 | tf_op jit(solution)/shard_map/while/body/eval_jaxpr/ppermute | solution.py:18
  171.1 8.8 %collective-permute-start = (bf16[2,128,4,128]{3,1,2,0:T(8,128)(2,1)}, bf16[2,128,4,128]{3,1,2,0:T(8,128)(2,1)S(1)}, u32[]{:S(2)}, u32[]{:S(2)}) collective-permute-start(bf16[2,128,4,128]{3,1,2,0:T(8,128)(2,1)} %get-tuple-element.1084), channel_id=1, source_target_pairs={{1,0},{2,1},{3,2},{4,3},{5,4},{6,5},{7,6},{9,8},{10,9},{11,10},{12... | collective-permute-start | bytes 786440 | tf_op jit(solution)/shard_map/while/body/eval_jaxpr/ppermute | solution.py:18
  188.5 85.7 %copy-start.18 = (f32[256]{0:T(256)S(1)}, f32[256]{0:T(256)}, u32[]{:S(2)}) copy-start(f32[256]{0:T(256)} %get-tuple-element.817) | copy-start | bytes 3076
  188.5 125.1 %copy-start.14 = (f32[128]{0:T(128)S(1)}, f32[128]{0:T(128)}, u32[]{:S(2)}) copy-start(f32[128]{0:T(128)} %copy-done.13) | copy-start | bytes 1540
  188.5 125.1 %copy-start.16 = (f32[128]{0:T(128)S(1)}, f32[128]{0:T(128)}, u32[]{:S(2)}) copy-start(f32[128]{0:T(128)} %copy-done.15) | copy-start | bytes 1540
  188.5 130.2 %reduce-scatter.19.cloned.1.call-start = ((), (), s32[]{:S(2)}) async-start(), calls=%async_computation.13 | async-start | bytes 163840
  190.3 128.4 %reduce-scatter.15.cloned.1.call-start = ((), (), s32[]{:S(2)}) async-start(), calls=%async_computation.11 | async-start | bytes 327680 | tf_op jit(solution)/shard_map/reduce_scatter | solution.py:216
  191.0 154.2 %reduce-scatter.11.cloned.1.call-start = ((), (), s32[]{:S(2)}) async-start(), calls=%async_computation.9 | async-start | bytes 1310720 | tf_op jit(solution)/shard_map/reduce_scatter | solution.py:215
Sparse Core Ops, SparseCore 0:
  14.7 26.1 all-gather.2
  42.8 23.4 all-gather.4
  87.5 36.0 reduce-scatter.16
  126.8 43.4 reduce-scatter.12
  188.6 85.4 reduce-scatter.8
  276.8 19.1 reduce-scatter.18
  299.0 17.8 reduce-scatter.14
  319.7 25.4 reduce-scatter.10
where the time goes:
time: 353 us; the launch traced here: 352 us
  waiting for transfers between devices  190 us (54%)
  matrix products  50 us (14%)
  blocking collectives  39.4 us (11%)
  other arithmetic  24.2 us (7%)
  local copies, waits for them, and re-layouts  21.5 us (6%)
  between operations  14.5 us (4%)
  starting transfers between devices  9.5 us (3%)
    reduce_scatter x1, waiting for transfers between devices, on_device(): lax.psum_scatter(in_part, 'seq', scatter_dimension=0, tiled=True)  83.1 us
    psum x1, blocking collectives, on_device(): d_head = lax.psum(head_part, ('dp', 'seq'))  39.4 us
    ppermute x7, waiting for transfers between devices, shifted(): return lax.ppermute(x, axis, pairs)  34.2 us
    reduce_scatter x1, waiting for transfers between devices, on_device(): lax.psum_scatter(partial_sums[0], 'dp', scatter_dimension=1, tiled=True)  26.5 us
    all_gather x1, waiting for transfers between devices, on_device(): lax.all_gather(key_b, 'seq', axis=0, tiled=True)  25.4 us
    all_gather x1, waiting for transfers between devices, on_device(): lax.all_gather(value_b, 'seq', axis=0, tiled=True)  19.6 us
    and x12, other arithmetic, visible(): return (same_hist & causal & open_key)[None, :, :]  11.7 us
    dot_general x8, matrix products, key_terms(): jnp.einsum('hrc,rhd->chd', d_raw_b, query_piece, preferred_element_type=j...  10.8 us
  transfers between devices with their start and end apart: 15, of which 11 were waited for; matrix products, arithmetic and copies ran while one was open for 20% of the time, Pallas kernels for 0%

commit v1 on v0

--- a/solution.py
+++ b/solution.py
@@ -1,5 +1,3 @@
-import math
-
 import jax
 import jax.numpy as jnp
 from jax import lax
@@ -10,12 +8,6 @@
 
 
 NORM_EPS = 1e-05
-
-
-def shifted(x, axis, by):
-    length = lax.axis_size(axis)
-    pairs = [(i, i + by) for i in range(length) if 0 <= i + by < length]
-    return lax.ppermute(x, axis, pairs)
 
 
 def silu_slope(value):
@@ -90,42 +82,13 @@
     value_b = hidden_b[:, width : 2 * width].reshape(rows, HEADS, DH)
     query_b = hidden_b[:, 2 * width : 3 * width].reshape(rows, HEADS, DH)
     key_b = hidden_b[:, 3 * width : 4 * width].reshape(rows, HEADS, DH)
-    key_all, value_all = (
-        lax.all_gather(key_b, "seq", axis=0, tiled=True),
-        lax.all_gather(value_b, "seq", axis=0, tiled=True),
+    moved = lax.all_gather(hidden_b[:, width:], "seq", axis=0, tiled=True)
+    value_all, query_all, key_all = (
+        moved[:, at * width : (at + 1) * width].reshape(total, HEADS, DH) for at in range(3)
     )
-    block_rows = math.gcd(512, total)
-    block_count = total // block_rows
-
-    def key_slice(array, number):
-        return lax.dynamic_slice_in_dim(array, number * block_rows, block_rows, 0)
-
-    def block_mask(number):
-        return visible(
-            positions,
-            segment,
-            key_slice(all_pos, number),
-            key_slice(all_seg, number),
-            key_slice(all_tgt, number),
-        )
-
-    def forward_step(carry, number):
-        raw_scores, attn_b = weights_of(
-            query_b, key_slice(key_all, number), block_mask(number), divisor
-        )
-        return (
-            carry
-            + jnp.einsum(
-                "hrc,chd->rhd",
-                attn_b,
-                key_slice(value_all, number),
-                preferred_element_type=jnp.float32,
-            ),
-            None,
-        )
-
-    numbers = jnp.arange(block_count, dtype=jnp.int32)
-    attended, unused = lax.scan(forward_step, jnp.zeros((rows, HEADS, DH), jnp.float32), numbers)
+    mask = visible(positions, segment, all_pos, all_seg, all_tgt)
+    raw_scores, attn_b = weights_of(query_b, key_all, mask, divisor)
+    attended = jnp.einsum("hrc,chd->rhd", attn_b, value_all, preferred_element_type=jnp.float32)
     attended = attended.reshape(rows, width)
     onorm, att_inverse = norm_rows(attended)
     gate_f = gate_b.astype(jnp.float32)
@@ -150,49 +113,14 @@
         .reshape(rows, HEADS, DH)
     )
 
-    def query_step(carry, number):
-        mask = block_mask(number)
-        raw_scores, attn_b = weights_of(query_b, key_slice(key_all, number), mask, divisor)
-        d_raw_b = score_grads(raw_scores, mask, d_att_b, key_slice(value_all, number), divisor)
-        return (
-            carry
-            + jnp.einsum(
-                "hrc,chd->rhd",
-                d_raw_b,
-                key_slice(key_all, number),
-                preferred_element_type=jnp.float32,
-            ),
-            None,
-        )
-
-    d_query, unused = lax.scan(query_step, jnp.zeros((rows, HEADS, DH), jnp.float32), numbers)
-
-    def key_terms(carry, query_piece, grad_piece, start):
-        piece_pos = start + jnp.arange(query_piece.shape[0], dtype=jnp.int32)
-        piece_seg, piece_tgt = row_marks(piece_pos, hist_len, hist_tgt)
-        mask = visible(piece_pos, piece_seg, positions, segment, target)
-        raw_scores, attn_b = weights_of(query_piece, key_b, mask, divisor)
-        d_raw_b = score_grads(raw_scores, mask, grad_piece, value_b, divisor)
-        d_key = carry[0] + jnp.einsum(
-            "hrc,rhd->chd", d_raw_b, query_piece, preferred_element_type=jnp.float32
-        )
-        d_value = carry[1] + jnp.einsum(
-            "hrc,rhd->chd", attn_b, grad_piece, preferred_element_type=jnp.float32
-        )
-        return (d_key, d_value)
-
-    empty = jnp.zeros((rows, HEADS, DH), jnp.float32)
-    own_terms = key_terms((empty, empty), query_b, d_att_b, own_start)
-
-    def later_pairs(step, state):
-        moving = shifted(state[0], "seq", -1)
-        start = own_start + step * rows
-        return (moving, key_terms(state[1], moving[0], moving[1], start))
-
-    final_state = lax.fori_loop(
-        1, seq_count, later_pairs, (jnp.stack([query_b, d_att_b]), own_terms)
-    )
-    d_key, d_value = final_state[1]
+    grad_all = lax.all_gather(d_att_b, "seq", axis=0, tiled=True)
+    d_raw_b = score_grads(raw_scores, mask, d_att_b, value_all, divisor)
+    d_query = jnp.einsum("hrc,chd->rhd", d_raw_b, key_all, preferred_element_type=jnp.float32)
+    key_mask = visible(all_pos, all_seg, positions, segment, target)
+    key_scores, key_attn_b = weights_of(query_all, key_b, key_mask, divisor)
+    key_raw_b = score_grads(key_scores, key_mask, grad_all, value_b, divisor)
+    d_key = jnp.einsum("hrc,rhd->chd", key_raw_b, query_all, preferred_element_type=jnp.float32)
+    d_value = jnp.einsum("hrc,rhd->chd", key_attn_b, grad_all, preferred_element_type=jnp.float32)
     d_hidden = jnp.concatenate(
         [
             d_gate,

time: 353 us -> 326 us (0.924)
  waiting for transfers between devices: 190 us -> 209 us
  other arithmetic: 24.2 us -> 5.79 us
  matrix products: 50 us -> 38.3 us
  starting transfers between devices: 9.5 us -> 0.51 us
    reduce_scatter x1, waiting for transfers between devices: 0.02 us -> 42.7 us  [on_device(): lax.psum_scatter(out_part, 'seq', scatter_dimension=0, tiled=True)]
    ppermute x7 -> x0, waiting for transfers between devices: 34.2 us -> none  [shifted(): return lax.ppermute(x, axis, pairs)]
    reduce_scatter x1, waiting for transfers between devices: 0.02 us -> 23.1 us  [on_device(): lax.psum_scatter(score_part, 'seq', scatter_dimension=0, tiled=True)]
    and x12 -> x2, other arithmetic: 11.7 us -> 0.5 us  [visible(): return (same_hist & causal & open_key)[None, :, :]]
    dot_general x20 -> x4, matrix products: 23.4 us -> 13.1 us  [the longest x1 4.3 us: on_device(): jnp.einsum('hrc,rhd->chd', key_raw_b, query_all, preferred_element_type=j...]
    ppermute x7 -> x0, starting transfers between devices: 9.18 us -> none  [shifted(): return lax.ppermute(x, axis, pairs)]
    reduce_scatter x1, waiting for transfers between devices: 83.1 us -> 75 us  [on_device(): lax.psum_scatter(in_part, 'seq', scatter_dimension=0, tiled=True)]
    dynamic_slice x16 -> x0, local copies, waits for them, and re-layouts: 7.39 us -> none  [the longest x12 5.04 us: key_slice(): return lax.dynamic_slice_in_dim(array, number * block_rows, block_rows, 0)]
  transfers between devices with their start and end apart: 15 -> 8, of which waited for: 11 -> 6; matrix products, arithmetic and copies ran while one was open for 20% -> 12% of each run, Pallas kernels for 0% -> 0%
where the time goes in v1:
time: 326 us; the launch traced here: 325 us
  waiting for transfers between devices  209 us (64%)
  blocking collectives  39.4 us (12%)
  matrix products  38.3 us (12%)
  local copies, waits for them, and re-layouts  18.1 us (6%)
  between operations  14.5 us (4%)
  other arithmetic  5.79 us (2%)
    reduce_scatter x1, waiting for transfers between devices, on_device(): lax.psum_scatter(in_part, 'seq', scatter_dimension=0, tiled=True)  75 us
    reduce_scatter x1, waiting for transfers between devices, on_device(): lax.psum_scatter(out_part, 'seq', scatter_dimension=0, tiled=True)  42.7 us
    psum x1, blocking collectives, on_device(): d_head = lax.psum(head_part, ('dp', 'seq'))  39.4 us
    all_gather x1, waiting for transfers between devices, on_device(): moved = lax.all_gather(hidden_b[:, width:], 'seq', axis=0, tiled=True)  33.1 us
    reduce_scatter x1, waiting for transfers between devices, on_device(): lax.psum_scatter(partial_sums[0], 'dp', scatter_dimension=1, tiled=True)  26.6 us
    reduce_scatter x1, waiting for transfers between devices, on_device(): lax.psum_scatter(score_part, 'seq', scatter_dimension=0, tiled=True)  23.1 us
    all_gather x1, waiting for transfers between devices, on_device(): grad_all = lax.all_gather(d_att_b, 'seq', axis=0, tiled=True)  8.2 us
  transfers between devices with their start and end apart: 8, of which 6 were waited for; matrix products, arithmetic and copies ran while one was open for 12% of the time, Pallas kernels for 0%

profile of v1, /device:TPU:0, one launch (start us, length us, event | category | flops | bytes accessed | tf_op | source)
XLA Modules:
  0.0 325.4 jit_solution(13088725939657065793)
XLA Ops:
  7.2 0.0 all-gather.3.cloned.1.call-start
  7.2 1.1 convert_reduce_fusion
  8.4 1.2 fusion.34
  9.6 4.1 %multiply_convert_fusion.2 = (bf16[128,2048]{1,0:T(8,128)(2,1)S(1)}, f32[128,2048]{1,0:T(8,128)}) fusion(bf16[1024,2048]{1,0:T(8,128)(2,1)} %param.12, bf16[1,128,1024]{2,1,0:T(8,128)(2,1)} %param.9, f32[128]{0:T(128)S(1)} %add_rsqrt_fusion.1, f32[128]{0:T(128)S(1)} %broadcast_multiply_fusion.5), kind=kOutput, calls=%fused_computation.25 | convolution fusion | flops 538705920 | bytes 6030336 | tf_op jit(solution)/shard_map/dot_general | solution.py:79
  13.7 0.8 slice.32
  14.5 0.0 all-gather.3.cloned.1.call-update
  14.5 0.0 all-gather.5.cloned.1.call-start
  14.6 0.2 reduce-window.4
  14.8 0.1 select_reduce_fusion
  14.9 0.1 select_reduce_fusion.1
  15.0 0.5 bitcast_select_fusion
  15.5 0.3 fusion.36
  15.8 0.8 slice_bitcast_fusion.1
  16.6 33.1 %all-gather.3.cloned.1.call-done = bf16[1024,1536]{1,0:T(8,128)(2,1)} async-done(((bf16[128,1536]{1,0:T(8,128)(2,1)}), bf16[1024,1536]{1,0:T(8,128)(2,1)}) %all-gather.3.cloned.1.call-update) | async-done | bytes 3145744 | tf_op jit(solution)/shard_map/all_gather | solution.py:85
  49.7 3.7 %fusion.87 = (bf16[1024,512]{1,0:T(8,128)(2,1)}, bf16[1024,512]{1,0:T(8,128)(2,1)}, bf16[128,4,8,128]{3,2,1,0:T(8,128)(2,1)}) fusion(bf16[1024,1536]{1,0:T(8,128)(2,1)} %all-gather.3.cloned.1.call-done), kind=kLoop, calls=%fused_computation.132 | loop fusion | bytes 6291456 | tf_op jit(solution)/shard_map/slice | solution.py:87
  53.4 1.5 copy.64
  54.9 0.4 fusion.53
  55.3 0.8 copy-done.7
  56.1 1.0 fusion.88
  57.1 0.1 fusion.44
  57.2 0.1 copy.58
  57.4 0.4 copy-done.17
  57.8 0.1 fusion.41
  57.9 0.3 fusion
  58.2 0.6 copy-done.8
  58.8 1.5 multiply_reduce_fusion.1
  60.3 0.6 copy-done.9
  60.9 1.0 convolution_add_fusion.1
  61.9 0.6 fusion.60
  62.5 0.9 fusion.45
  63.4 1.7 copy.65
  65.1 0.0 all-gather.5.cloned.1.call-update
  65.1 0.0 reduce-scatter.17.cloned.1.call-start
  65.2 2.3 fusion.85
  67.4 0.0 reduce-scatter.17.cloned.1.call-update
  67.5 0.0 reduce-scatter.13.cloned.1.call-start
  67.5 1.8 fusion.56
  69.4 0.0 reduce-scatter.13.cloned.1.call-update
  69.4 0.2 reduce-scatter.9.cloned.1.call-start
  69.7 0.2 fusion.39
  69.9 2.3 copy.66
  72.2 4.2 %fusion.1 = f32[4,128,128]{2,1,0:T(8,128)} fusion(bf16[1024,4,128]{0,2,1:T(8,128)(2,1)S(1)} %bitcast.120, f32[4,128,1024]{2,1,0:T(8,128)} %copy-done.5, bf16[128,4,128]{0,2,1:T(8,128)(2,1)S(1)} %bitcast.126, pred[128,1024]{1,0:T(8,128)(4,1)S(1)} %copy-done.14, bf16[128,4,8,128]{3,2,1,0:T(8,128)(2,1)} %get-tuple-element.30), kind=kOutput, calls=%fused_computation.9 | convolution fusion | flops 274726912 | bytes 4718592 | tf_op jit(solution)/shard_map/hrc,chd->rhd/dot_general | solution.py:118
  76.4 1.1 copy.60
  77.5 3.1 fusion.50
  80.6 8.2 %all-gather.5.cloned.1.call-done = bf16[1024,4,128]{0,2,1:T(8,128)(2,1)} async-done(((bf16[128,4,128]{0,2,1:T(8,128)(2,1)}), bf16[1024,4,128]{0,2,1:T(8,128)(2,1)}) %all-gather.5.cloned.1.call-update) | async-done | bytes 1048592 | tf_op jit(solution)/shard_map/all_gather | solution.py:116
  88.8 3.5 %fusion.19 = f32[4,128,128]{2,1,0:T(8,128)} fusion(bf16[1024,4,128]{0,2,1:T(8,128)(2,1)} %all-gather.5.cloned.1.call-done, f32[4,1024,128]{2,1,0:T(8,128)} %fusion.50, pred[1024,128]{1,0:T(8,128)(4,1)S(1)} %fusion.39), kind=kOutput, calls=%fused_computation.30 | convolution fusion | flops 138412032 | bytes 3538944 | tf_op jit(solution)/shard_map/hrc,rhd->chd/dot_general | solution.py:123
  92.4 1.1 copy.59
  93.5 4.3 %fusion.2 = f32[4,128,128]{2,1,0:T(8,128)} fusion(bf16[1024,4,128]{0,2,1:T(8,128)(2,1)S(1)} %bitcast.122, f32[4,1024,128]{2,1,0:T(8,128)} %fusion.50, bf16[1024,4,128]{0,2,1:T(8,128)(2,1)} %all-gather.5.cloned.1.call-done, pred[1024,128]{1,0:T(8,128)(4,1)S(1)} %fusion.39, bf16[16,4,8,128]{3,2,1,0:T(8,128)(2,1)} %get-tuple-element.33), kind=kOutput, calls=%fused_computation.10 | convolution fusion | flops 274726912 | bytes 4718592 | tf_op jit(solution)/shard_map/hrc,rhd->chd/dot_general | solution.py:122
  97.8 1.1 copy.61
  98.9 6.0 %fusion.81 = f32[1024,2048]{1,0:T(8,128)} fusion(bf16[1,128,1024]{2,1,0:T(8,128)(2,1)S(1)} %copy-done.1, f32[128]{0:T(128)S(1)} %copy-done.20, f32[128]{0:T(128)S(1)} %broadcast_multiply_fusion.5, f32[128,512]{1,0:T(8,128)S(1)} %copy.61, f32[128,512]{1,0:T(8,128)S(1)} %copy.60, f32[128,512]{1,0:T(8,128)S(1)} %copy.59, f32[128,512]{1,0:T(8,128)} %get-tuple-element.31, ...), kind=kOutput, calls=%fused_computation.128 | convolution fusion | flops 540540928 | bytes 10748928 | tf_op jit(solution)/shard_map/dot_general | solution.py:134
  104.9 0.0 reduce-scatter.9.cloned.1.call-update
  104.9 0.0 reduce-scatter.19.cloned.1.call-start
  104.9 23.1 %reduce-scatter.17.cloned.1.call-done = f32[128,256]{1,0:T(8,128)} async-done(((f32[1024,256]{1,0:T(8,128)}), f32[128,256]{1,0:T(8,128)}) %reduce-scatter.17.cloned.1.call-update) | async-done | bytes 131088 | tf_op jit(solution)/shard_map/reduce_scatter | solution.py:140
  128.1 1.7 copy.62
  129.7 0.0 reduce-scatter.19.cloned.1.call-update
  129.7 0.0 reduce-scatter.15.cloned.1.call-start
  129.8 42.7 %reduce-scatter.13.cloned.1.call-done = f32[64,1024]{1,0:T(8,128)} async-done(((f32[512,1024]{1,0:T(8,128)}), f32[64,1024]{1,0:T(8,128)}) %reduce-scatter.13.cloned.1.call-update) | async-done | bytes 262160 | tf_op jit(solution)/shard_map/reduce_scatter | solution.py:139
  172.5 0.0 reduce-scatter.15.cloned.1.call-update
  172.5 0.0 reduce-scatter.11.cloned.1.call-start
  172.5 75.0 %reduce-scatter.9.cloned.1.call-done = f32[128,2048]{1,0:T(8,128)} async-done(((f32[1024,2048]{1,0:T(8,128)}), f32[128,2048]{1,0:T(8,128)}) %reduce-scatter.9.cloned.1.call-update) | async-done | bytes 1048592 | tf_op jit(solution)/shard_map/reduce_scatter | solution.py:138
  247.5 39.4 %psum.7 = f32[256]{0:T(256)} all-reduce(f32[256]{0:T(256)S(1)} %copy-done.23), channel_id=1, replica_groups=mesh['dp'=4,'seq'=8] {'dp','seq'}, use_global_device_ids=true, to_apply=%region_20.21 | all-reduce | flops 256 | bytes 2048 | tf_op jit(solution)/shard_map/psum | solution.py:147
  286.9 4.1 %fusion.86 = (f32[128]{0:T(128)S(1)}, f32[128]{0:T(128)S(1)}, f32[128,1024]{1,0:T(8,128)S(1)}) fusion(f32[128]{0:T(128)S(1)} %copy-done.20, f32[128]{0:T(128)S(1)} %broadcast_multiply_fusion.5, bf16[1,128,1024]{2,1,0:T(8,128)(2,1)S(1)} %copy-done.1, bf16[1024,2048]{1,0:T(8,128)(2,1)} %param.12, f32[128,512]{1,0:T(8,128)S(1)} %copy.61, ...), kind=kOutput, calls=%fused_computation.131 | convolution fusion | flops 540802816 | bytes 7079936 | tf_op jit(solution)/shard_map/dot_general | solution.py:135
  291.0 1.0 fusion.42
  292.0 26.6 %reduce-scatter.11.cloned.1.call-done = f32[128,512]{1,0:T(8,128)} async-done(((f32[128,2048]{1,0:T(8,128)}), f32[128,512]{1,0:T(8,128)}) %reduce-scatter.11.cloned.1.call-update) | async-done | bytes 262160 | tf_op jit(solution)/shard_map/reduce_scatter | solution.py:143
  (64 shorter events, 0.2 us)
Async XLA Ops:
  7.2 50.7 %copy-start = (bf16[512,1024]{1,0:T(8,128)(2,1)S(1)}, bf16[512,1024]{1,0:T(8,128)(2,1)}, u32[]{:S(2)}) copy-start(bf16[512,1024]{1,0:T(8,128)(2,1)} %param.13) | copy-start | bytes 3145732
  7.2 42.5 %all-gather.3.cloned.1.call-start = ((), (), s32[]{:S(2)}) async-start(), calls=%async_computation.6 | async-start | bytes 3538944 | tf_op jit(solution)/shard_map/all_gather | solution.py:85
  9.6 4.1 %copy-start.19 = (f32[128]{0:T(128)}, f32[128]{0:T(128)S(1)}, u32[]{:S(2)}) copy-start(f32[128]{0:T(128)S(1)} %add_rsqrt_fusion.1) | copy-start | bytes 1540
  9.6 5.0 %copy-start.24 = (s32[1,8]{1,0:T(1,128)S(1)}, s32[1,8]{1,0:T(1,128)}, u32[]{:S(2)}) copy-start(s32[1,8]{1,0:T(1,128)} %param.10) | copy-start | bytes 100
  9.6 5.2 %copy-start.25 = (s32[1,8]{1,0:T(1,128)S(1)}, s32[1,8]{1,0:T(1,128)}, u32[]{:S(2)}) copy-start(s32[1,8]{1,0:T(1,128)} %param.11) | copy-start | bytes 100
  9.6 5.4 %copy-start.26 = (f32[1,128]{1,0:T(1,128)S(1)}, f32[1,128]{1,0:T(1,128)}, u32[]{:S(2)}) copy-start(f32[1,128]{1,0:T(1,128)} %param.17) | copy-start | bytes 1540
  13.7 43.7 %copy-start.3 = (bf16[128,2048]{1,0:T(8,128)(2,1)}, bf16[128,2048]{1,0:T(8,128)(2,1)S(1)}, u32[]{:S(2)}) copy-start(bf16[128,2048]{1,0:T(8,128)(2,1)S(1)} %get-tuple-element.38) | copy-start | bytes 1572868
  14.5 74.3 %all-gather.5.cloned.1.call-start = ((), (), s32[]{:S(2)}) async-start(), calls=%async_computation.7 | async-start | bytes 1179648 | tf_op jit(solution)/shard_map/all_gather | solution.py:116
  15.0 0.6 copy-start.21
  15.0 38.4 %copy-start.15 = (s32[128]{0:T(128)}, s32[128]{0:T(128)S(1)}, u32[]{:S(2)}) copy-start(s32[128]{0:T(128)S(1)} %get-tuple-element.25) | copy-start | bytes 1540
  15.8 39.5 %copy-start.13 = (pred[128,1024]{1,0:T(8,128)(4,1)}, pred[128,1024]{1,0:T(8,128)(4,1)S(1)}, u32[]{:S(2)}) copy-start(pred[128,1024]{1,0:T(8,128)(4,1)S(1)} %fusion.36) | copy-start | bytes 393220
  54.9 1.2 copy-start.7
  55.3 1.8 copy-start.5
  56.1 1.8 copy-start.1
  57.2 0.5 copy-start.17
  57.7 1.0 copy-start.8
  57.8 3.2 copy-start.12
  57.9 4.0 %copy-start.4 = (bf16[128,2048]{1,0:T(8,128)(2,1)S(1)}, bf16[128,2048]{1,0:T(8,128)(2,1)}, u32[]{:S(2)}) copy-start(bf16[128,2048]{1,0:T(8,128)(2,1)} %copy-done.3) | copy-start | bytes 1572868
  57.9 4.0 %copy-start.18 = (f32[128]{0:T(128)S(1)}, f32[128]{0:T(128)}, u32[]{:S(2)}) copy-start(f32[128]{0:T(128)} %copy-done.17) | copy-start | bytes 1540
  60.3 0.6 copy-start.9
  65.1 63.0 %reduce-scatter.17.cloned.1.call-start = ((), (), s32[]{:S(2)}) async-start(), calls=%async_computation.12 | async-start | bytes 1179648 | tf_op jit(solution)/shard_map/reduce_scatter | solution.py:140
  67.4 2.2 copy-start.22
  67.4 2.2 copy-start.16
  67.5 105.0 %reduce-scatter.13.cloned.1.call-start = ((), (), s32[]{:S(2)}) async-start(), calls=%async_computation.10 | async-start | bytes 2359296 | tf_op jit(solution)/shard_map/reduce_scatter | solution.py:139
  69.4 2.8 copy-start.11
  69.4 2.8 copy-start.14
  69.4 178.1 %reduce-scatter.9.cloned.1.call-start = ((), (), s32[]{:S(2)}) async-start(), calls=%async_computation.8 | async-start | bytes 9437184 | tf_op jit(solution)/shard_map/reduce_scatter | solution.py:138
  72.2 5.3 %copy-start.10 = (bf16[16,4,8,128]{3,2,1,0:T(8,128)(2,1)S(1)}, bf16[16,4,8,128]{3,2,1,0:T(8,128)(2,1)}, u32[]{:S(2)}) copy-start(bf16[16,4,8,128]{3,2,1,0:T(8,128)(2,1)} %get-tuple-element.34) | copy-start | bytes 393220
  80.6 12.8 %copy-start.2 = (bf16[1024,512]{0,1:T(8,128)(2,1)S(1)}, bf16[1024,512]{0,1:T(8,128)(2,1)}, u32[]{:S(2)}) copy-start(bf16[1024,512]{0,1:T(8,128)(2,1)} %copy.66) | copy-start | bytes 3145732
  93.4 5.4 %copy-start.20 = (f32[128]{0:T(128)S(1)}, f32[128]{0:T(128)}, u32[]{:S(2)}) copy-start(f32[128]{0:T(128)} %copy-done.19) | copy-start | bytes 1540
  104.9 142.6 %copy-start.23 = (f32[256]{0:T(256)S(1)}, f32[256]{0:T(256)}, u32[]{:S(2)}) copy-start(f32[256]{0:T(256)} %get-tuple-element.44) | copy-start | bytes 3076
  104.9 182.0 %copy-start.6 = (f32[128,512]{1,0:T(8,128)S(1)}, f32[128,512]{1,0:T(8,128)}, u32[]{:S(2)}) copy-start(f32[128,512]{1,0:T(8,128)} %get-tuple-element.31) | copy-start | bytes 786436
  104.9 187.1 %reduce-scatter.19.cloned.1.call-start = ((), (), s32[]{:S(2)}) async-start(), calls=%async_computation.13 | async-start | bytes 163840
  129.7 162.2 %reduce-scatter.15.cloned.1.call-start = ((), (), s32[]{:S(2)}) async-start(), calls=%async_computation.11 | async-start | bytes 327680 | tf_op jit(solution)/shard_map/reduce_scatter | solution.py:144
  172.5 146.1 %reduce-scatter.11.cloned.1.call-start = ((), (), s32[]{:S(2)}) async-start(), calls=%async_computation.9 | async-start | bytes 1310720 | tf_op jit(solution)/shard_map/reduce_scatter | solution.py:143
Sparse Core Ops, SparseCore 0:
  14.7 35.0 all-gather.2
  65.2 23.5 all-gather.4
  92.0 36.0 reduce-scatter.16
  131.2 41.1 reduce-scatter.12
  176.2 71.2 reduce-scatter.8
  250.1 19.1 reduce-scatter.18
  272.3 17.9 reduce-scatter.14
  293.2 25.3 reduce-scatter.10

commit v2 on v1

--- a/solution.py
+++ b/solution.py
@@ -1,6 +1,10 @@
+import functools
+
 import jax
 import jax.numpy as jnp
 from jax import lax
+from jax.experimental import pallas as pl
+from jax.experimental.pallas import tpu as pltpu
 from jax.sharding import PartitionSpec as P
 
 HEADS = 4
@@ -8,6 +12,121 @@
 
 
 NORM_EPS = 1e-05
+
+
+def exchange_kernel(plan, *refs):
+    count = len(plan)
+    sources, targets = refs[:count], refs[count : 2 * count]
+    send_sems, recv_sems, own_sems = refs[2 * count :]
+    axes = sorted({axis for kind, axis in plan})
+    barrier = pltpu.get_barrier_semaphore()
+    for axis in axes:
+        size, me = lax.axis_size(axis), lax.axis_index(axis)
+        for step in range(1, size):
+            pl.semaphore_signal(
+                barrier,
+                inc=1,
+                device_id={axis: lax.rem(me + step, size)},
+                device_id_type=pl.DeviceIdType.MESH,
+            )
+    pl.semaphore_wait(barrier, sum(lax.axis_size(axis) - 1 for axis in axes))
+
+    def remote(source, target, number, slot, axis, peer):
+        return pltpu.make_async_remote_copy(
+            src_ref=source,
+            dst_ref=target,
+            send_sem=send_sems.at[number, slot],
+            recv_sem=recv_sems.at[number, slot],
+            device_id={axis: peer},
+            device_id_type=pl.DeviceIdType.MESH,
+        )
+
+    sent, own, relays, landing = [], [], [], []
+    for number, (kind, axis) in enumerate(plan):
+        source, target = sources[number], targets[number]
+        size, me = lax.axis_size(axis), lax.axis_index(axis)
+        mine = source if kind == "gather" else source.at[me]
+        own.append(pltpu.make_async_copy(mine, target.at[me], own_sems.at[number]))
+        own[-1].start()
+        if kind == "gather":
+            sibling = me + 1 - 2 * lax.rem(me, 2)
+            for step in range(1, size // 2):
+                copy = remote(
+                    source, target.at[me], number, step, axis, lax.rem(me + 2 * step, size)
+                )
+                copy.start()
+                sent.append(copy)
+                relays.append((number, axis, step, lax.rem(me + size - 2 * step, size), sibling))
+            copy = remote(source, target.at[me], number, 0, axis, sibling)
+            copy.start()
+            sent.append(copy)
+            landing.append(remote(source, target.at[sibling], number, 0, axis, sibling))
+            for step in range(1, size // 2):
+                origin = lax.rem(sibling + size - 2 * step, size)
+                landing.append(
+                    remote(source, target.at[origin], number, size // 2 + step, axis, sibling)
+                )
+        else:
+            for step in range(1, size):
+                peer = lax.rem(me + step, size)
+                copy = remote(source.at[peer], target.at[me], number, step, axis, peer)
+                copy.start()
+                sent.append(copy)
+                origin = lax.rem(me + size - step, size)
+                landing.append(
+                    remote(source.at[origin], target.at[origin], number, step, axis, origin)
+                )
+    for number, axis, step, origin, sibling in relays:
+        size = lax.axis_size(axis)
+        block = targets[number].at[origin]
+        remote(sources[number], block, number, step, axis, origin).wait_recv()
+        copy = remote(block, block, number, size // 2 + step, axis, sibling)
+        copy.start()
+        sent.append(copy)
+    for copy in landing:
+        copy.wait_recv()
+    for copy in sent:
+        copy.wait_send()
+    for copy in own:
+        copy.wait()
+
+
+def exchange(identity, *items):
+    plan = tuple((kind, axis) for kind, axis, array in items)
+    arrays = [array for kind, axis, array in items]
+    shapes = [
+        jax.ShapeDtypeStruct(
+            ((lax.axis_size(axis),) + array.shape) if kind == "gather" else array.shape,
+            array.dtype,
+        )
+        for kind, axis, array in items
+    ]
+    slots = max(lax.axis_size(axis) for kind, axis in plan)
+    return pl.pallas_call(
+        functools.partial(exchange_kernel, plan),
+        out_shape=shapes,
+        in_specs=[pl.BlockSpec(memory_space=pl.ANY)] * len(arrays),
+        out_specs=[pl.BlockSpec(memory_space=pl.ANY)] * len(arrays),
+        scratch_shapes=[
+            pltpu.SemaphoreType.DMA((len(arrays), slots)),
+            pltpu.SemaphoreType.DMA((len(arrays), slots)),
+            pltpu.SemaphoreType.DMA((len(arrays),)),
+        ],
+        compiler_params=pltpu.CompilerParams(collective_id=identity, has_side_effects=True),
+    )(*arrays)
+
+
+def blocks(array, count):
+    rows, columns = array.shape
+    return array.reshape(rows, count, columns // count).transpose(1, 0, 2)
+
+
+def merged(array):
+    return array.reshape(array.shape[0] * array.shape[1], array.shape[2])
+
+
+def group_sum(array):
+    return jnp.sum(array.astype(jnp.float32), axis=0)
 
 
 def silu_slope(value):
@@ -82,7 +201,12 @@
     value_b = hidden_b[:, width : 2 * width].reshape(rows, HEADS, DH)
     query_b = hidden_b[:, 2 * width : 3 * width].reshape(rows, HEADS, DH)
     key_b = hidden_b[:, 3 * width : 4 * width].reshape(rows, HEADS, DH)
-    moved = lax.all_gather(hidden_b[:, width:], "seq", axis=0, tiled=True)
+    moved, normed_cols = exchange(
+        1,
+        ("gather", "seq", hidden_b[:, width:]),
+        ("swap", "seq", blocks(normed_b, seq_count)),
+    )
+    moved = merged(moved)
     value_all, query_all, key_all = (
         moved[:, at * width : (at + 1) * width].reshape(total, HEADS, DH) for at in range(3)
     )
@@ -99,12 +223,10 @@
     weight_c = grad_score[0] * target.astype(jnp.float32)
     head_part = jnp.sum(weight_c[:, None] * jax.nn.silu(mid_act), axis=0)
     d_mid_b = (weight_c[:, None] * head_score[None, :] * silu_slope(mid_act)).astype(jnp.bfloat16)
-    score_part = jnp.dot(out_b.T, d_mid_b, preferred_element_type=jnp.float32)
     d_total = grad_out[0].astype(jnp.float32) + jnp.dot(
         d_mid_b, w_score.T, preferred_element_type=jnp.float32
     )
     d_total_b = d_total.astype(jnp.bfloat16)
-    out_part = jnp.dot(gated_b.T, d_total_b, preferred_element_type=jnp.float32)
     d_gated = jnp.dot(d_total_b, w_out.T, preferred_element_type=jnp.float32)
     d_gate = d_gated * onorm
     d_att_b = (
@@ -113,7 +235,21 @@
         .reshape(rows, HEADS, DH)
     )
 
-    grad_all = lax.all_gather(d_att_b, "seq", axis=0, tiled=True)
+    grad_all, total_all, mid_all, head_all, gated_cols, out_cols = exchange(
+        2,
+        ("gather", "seq", d_att_b.reshape(rows, width)),
+        ("gather", "seq", d_total_b),
+        ("gather", "seq", d_mid_b),
+        ("gather", "seq", jnp.broadcast_to(head_part, (8, head_part.shape[0]))),
+        ("swap", "seq", blocks(gated_b, seq_count)),
+        ("swap", "seq", blocks(out_b, seq_count)),
+    )
+    grad_all = grad_all.reshape(total, HEADS, DH)
+    out_part = jnp.dot(
+        merged(gated_cols).T, merged(total_all), preferred_element_type=jnp.float32
+    )
+    score_part = jnp.dot(merged(out_cols).T, merged(mid_all), preferred_element_type=jnp.float32)
+    head_group = jnp.sum(head_all, axis=0)
     d_raw_b = score_grads(raw_scores, mask, d_att_b, value_all, divisor)
     d_query = jnp.einsum("hrc,chd->rhd", d_raw_b, key_all, preferred_element_type=jnp.float32)
     key_mask = visible(all_pos, all_seg, positions, segment, target)
@@ -131,21 +267,25 @@
         axis=1,
     )
     d_pre_b = (d_hidden * silu_slope(pre_act)).astype(jnp.bfloat16)
-    in_part = jnp.dot(normed_b.T, d_pre_b, preferred_element_type=jnp.float32)
+    group_count = lax.axis_size("dp")
+    pre_all, out_parts, score_parts, head_parts = exchange(
+        3,
+        ("gather", "seq", d_pre_b),
+        ("swap", "dp", blocks(out_part.astype(jnp.bfloat16), group_count)),
+        ("swap", "dp", blocks(score_part.astype(jnp.bfloat16), group_count)),
+        ("swap", "dp", jnp.broadcast_to(head_group, (group_count,) + head_group.shape)),
+    )
+    in_part = jnp.dot(merged(normed_cols).T, merged(pre_all), preferred_element_type=jnp.float32)
+    (in_parts,) = exchange(4, ("swap", "dp", blocks(in_part.astype(jnp.bfloat16), group_count)))
     d_normed = jnp.dot(d_pre_b, w_in.T, preferred_element_type=jnp.float32)
     d_x = (d_total + norm_back(d_normed, normed, inverse)).astype(jnp.bfloat16)
-    partial_sums = (
-        lax.psum_scatter(in_part, "seq", scatter_dimension=0, tiled=True),
-        lax.psum_scatter(out_part, "seq", scatter_dimension=0, tiled=True),
-        lax.psum_scatter(score_part, "seq", scatter_dimension=0, tiled=True),
-    )
-    d_w_in, d_w_out, d_w_score = (
-        lax.psum_scatter(partial_sums[0], "dp", scatter_dimension=1, tiled=True),
-        lax.psum_scatter(partial_sums[1], "dp", scatter_dimension=1, tiled=True),
-        lax.psum_scatter(partial_sums[2], "dp", scatter_dimension=1, tiled=True),
-    )
-    d_head = lax.psum(head_part, ("dp", "seq"))
-    return (d_x[None], d_w_in, d_w_out, d_w_score, d_head)
+    return (
+        d_x[None],
+        group_sum(in_parts),
+        group_sum(out_parts),
+        group_sum(score_parts),
+        group_sum(head_parts)[0],
+    )
 
 
 def solution(mesh):

time: 326 us -> 184 us (0.56)
  waiting for transfers between devices: 209 us -> 0 us
  Pallas kernels: 0 us -> 101 us
  blocking collectives: 39.4 us -> 0 us
  between operations: 14.5 us -> 1.03 us
  other arithmetic: 5.79 us -> 17.1 us
  local copies, waits for them, and re-layouts: 18.1 us -> 28.7 us
    reduce_scatter x5 -> x0, waiting for transfers between devices: 167 us -> none  [the longest x1 75 us: on_device(): lax.psum_scatter(in_part, 'seq', scatter_dimension=0, tiled=True)]
    pallas_call x0 -> x4, Pallas kernels: none -> 101 us  [exchange(): pl.pallas_call(functools.partial(exchange_kernel, plan), out_shape=shapes...]
    all_gather x2 -> x0, waiting for transfers between devices: 41.3 us -> none  [the longest x1 33.1 us: on_device(): moved = lax.all_gather(hidden_b[:, width:], 'seq', axis=0, tiled=True)]
    psum x1 -> x0, blocking collectives: 39.4 us -> none  [on_device(): d_head = lax.psum(head_part, ('dp', 'seq'))]
    dot_general x3, matrix products: 10.1 us -> 6.34 us  [the longest x1 2.93 us: on_device(): jnp.dot(merged(normed_cols).T, merged(pre_all), preferred_element_type=jn...]
    reshape x3 -> x6, local copies, waits for them, and re-layouts: 5.43 us -> 7.27 us  [the longest x5 5.1 us: blocks(): return array.reshape(rows, count, columns // count).transpose(1, 0, 2)]
  transfers between devices with their start and end apart: 8 -> 0, of which waited for: 6 -> 0; matrix products, arithmetic and copies ran while one was open for 12% -> 0% of each run, Pallas kernels for 0% -> 0%
where the time goes in v2:
time: 184 us
  Pallas kernels  101 us (55%)
  matrix products  35.5 us (19%)
  local copies, waits for them, and re-layouts  28.7 us (16%)
  other arithmetic  17.1 us (9%)
    pallas_call x4, Pallas kernels, exchange(): pl.pallas_call(functools.partial(exchange_kernel, plan), out_shape=shapes...  101 us
    unnamed x53, local copies, waits for them, and re-layouts  6.38 us
    slice x2, local copies, waits for them, and re-layouts, on_device(): moved[:, at * width:(at + 1) * width].reshape(total, HEADS, DH)  5.71 us
    reshape x5, local copies, waits for them, and re-layouts, blocks(): return array.reshape(rows, count, columns // count).transpose(1, 0, 2)  5.1 us
    dot_general x1, matrix products, on_device(): jnp.einsum('hrc,chd->rhd', d_raw_b, key_all, preferred_element_type=jnp.f...  4.23 us
    dot_general x1, matrix products, on_device(): jnp.einsum('hrc,rhd->chd', key_raw_b, query_all, preferred_element_type=j...  4.11 us
    dot_general x1, matrix products, on_device(): pre_act = jnp.dot(normed_b, w_in, preferred_element_type=jnp.float32)  3.98 us
    dot_general x1, matrix products, on_device(): d_normed = jnp.dot(d_pre_b, w_in.T, preferred_element_type=jnp.float32)  3.84 us

profile of v2, /device:TPU:0, one launch (start us, length us, event | category | flops | bytes accessed | tf_op | source)
XLA Modules:
  0.0 183.5 jit_solution(18278358892123253389)
XLA Ops:
  0.7 0.9 reduce-window.4
  1.6 1.1 convert_reduce_fusion.1
  2.7 1.2 fusion.33
  3.9 0.7 fusion.69
  4.6 1.2 bitcast_select_fusion
  5.9 0.9 fusion.37
  6.8 0.9 fusion.40
  7.7 1.0 convert_bitcast_fusion
  8.7 0.1 copy.131
  8.8 1.0 fusion.43.refs_1_
  9.9 4.0 %multiply_convert_fusion.2 = (bf16[128,2048]{1,0:T(8,128)(2,1)S(1)}, f32[128,2048]{1,0:T(8,128)}) fusion(bf16[1024,2048]{1,0:T(8,128)(2,1)} %param.12, bf16[1,128,1024]{2,1,0:T(8,128)(2,1)S(1)} %copy-done.1, f32[128]{0:T(128)S(1)} %add_rsqrt_fusion.1, f32[128]{0:T(128)S(1)} %broadcast_multiply_fusion.5), kind=kOutput, calls=%fused_computation.28 | convolution fusion | flops 538705920 | bytes 6030336 | tf_op jit(solution)/shard_map/dot_general | solution.py:198
  13.8 0.8 slice.36.refs_0_
  14.7 0.1 copy-done.4
  14.8 0.7 slice_bitcast_fusion
  15.5 25.7 %shard_map.128 = (bf16[8,128,1536]{2,1,0:T(8,128)(2,1)}, bf16[8,128,128]{2,1,0:T(8,128)(2,1)}) custom-call(bf16[128,1536]{1,0:T(8,128)(2,1)} %slice.36.refs_0_, bf16[8,128,128]{2,1,0:T(8,128)(2,1)} %fusion.43.refs_1_), custom_call_target="tpu_custom_call" | custom-call | tf_op jit(solution)/shard_map/pallas_call | solution.py:105
  41.2 3.4 %fusion.88 = (bf16[1024,512]{1,0:T(8,128)(2,1)S(1)}, bf16[1024,512]{1,0:T(8,128)(2,1)}, bf16[1024,512]{1,0:T(8,128)(2,1)}) fusion(bf16[1024,1536]{1,0:T(8,128)(2,1)} %bitcast.160), kind=kLoop, calls=%fused_computation.141 | loop fusion | bytes 6291456 | tf_op jit(solution)/shard_map/slice | solution.py:211
  44.6 0.5 copy.125
  45.2 1.5 copy.124
  46.7 2.3 %copy.85 = bf16[1024,512]{0,1:T(8,128)(2,1)} copy(bf16[1024,512]{1,0:T(8,128)(2,1)} %get-tuple-element.49) | data formatting | bytes 2097152 | tf_op jit(solution)/shard_map/slice | solution.py:211
  49.0 0.4 fusion.63
  49.4 0.8 copy-done.8
  50.2 0.9 fusion.89
  51.1 0.4 copy-done.7
  51.5 0.7 copy-done.10
  52.3 1.8 copy.120
  54.1 1.1 fusion.42
  55.2 0.7 copy.90
  56.0 0.3 fusion.1
  56.3 0.7 copy-done.11
  57.0 2.6 %multiply_reduce_fusion.1 = (f32[256]{0:T(256)}, bf16[128,256]{1,0:T(8,128)(2,1)}) fusion(f32[128]{0:T(128)} %bitcast_select_fusion, f32[256]{0:T(256)} %param.15, bf16[128,1024]{1,0:T(8,128)(2,1)S(1)} %fusion.1, bf16[1024,256]{1,0:T(8,128)(2,1)} %param.14), kind=kOutput, calls=%fused_computation.95 | convolution fusion | flops 67534592 | bytes 854528 | tf_op jit(solution)/shard_map/dot_general | solution.py:222
  59.6 1.8 copy.92
  61.4 1.8 copy.93
  63.2 1.3 broadcast_in_dim.67.refs_3_
  64.5 0.9 copy.91
  65.3 2.3 %fusion.90 = (bf16[128,1024]{1,0:T(8,128)(2,1)S(1)}, f32[128,1024]{1,0:T(8,128)}) fusion(bf16[128,256]{1,0:T(8,128)(2,1)} %get-tuple-element.56.refs_2_, bf16[1024,256]{1,0:T(8,128)(2,1)} %param.14, bf16[1,128,1024]{2,1,0:T(8,128)(2,1)} %param.16), kind=kOutput, calls=%fused_computation.143 | convolution fusion | flops 67502080 | bytes 1638400 | tf_op jit(solution)/shard_map/dot_general | solution.py:226
  67.6 1.7 fusion.66
  69.3 1.8 fusion.51
  71.1 4.2 %fusion.2 = f32[4,128,128]{2,1,0:T(8,128)} fusion(bf16[1024,4,128]{0,2,1:T(8,128)(2,1)S(1)} %bitcast.159, f32[4,128,1024]{2,1,0:T(8,128)} %copy-done.7, bf16[1024,4,128]{0,2,1:T(8,128)(2,1)} %bitcast.164, pred[128,1024]{1,0:T(8,128)(4,1)} %fusion.37, bf16[128,512]{1,0:T(8,128)(2,1)} %get-tuple-element.51.refs_0_), kind=kOutput, calls=%fused_computation.11 | convolution fusion | flops 274726912 | bytes 4718592 | tf_op jit(solution)/shard_map/hrc,chd->rhd/dot_general | solution.py:254
  75.3 1.1 copy.122
  76.4 1.8 fusion.60
  78.2 30.7 %shard_map.129 = (bf16[8,128,512]{2,1,0:T(8,128)(2,1)}, bf16[8,128,1024]{2,1,0:T(8,128)(2,1)}, bf16[8,128,256]{2,1,0:T(8,128)(2,1)}, f32[8,8,256]{2,1,0:T(8,128)...) custom-call(bf16[128,512]{1,0:T(8,128)(2,1)} %get-tuple-element.51.refs_0_, bf16[128,1024]{1,0:T(8,128)(2,1)} %copy-done.5, ...), custom_call_target="tpu_custom_call" | custom-call | tf_op jit(solution)/shard_map/pallas_call | solution.py:105
  108.9 2.2 %reshape.350 = bf16[1024,4,128]{2,1,0:T(4,128)(2,1)} reshape(bf16[8,128,512]{2,1,0:T(8,128)(2,1)} %get-tuple-element.18) | data formatting | bytes 2097152 | tf_op jit(solution)/shard_map/reshape | solution.py:247
  111.1 4.1 %fusion.3 = f32[4,128,128]{2,1,0:T(8,128)} fusion(bf16[1024,4,128]{0,2,1:T(8,128)(2,1)S(1)} %bitcast.157, f32[4,1024,128]{2,1,0:T(8,128)} %fusion.60, pred[1024,128]{1,0:T(8,128)(4,1)S(1)} %copy-done.19, bf16[1024,4,128]{2,1,0:T(4,128)(2,1)} %reshape.350, bf16[16,4,8,128]{3,2,1,0:T(8,128)(2,1)S(1)} %copy-done.21), kind=kOutput, calls=%fused_computation.12 | convolution fusion | flops 274726912 | bytes 4718592 | tf_op jit(solution)/shard_map/hrc,rhd->chd/dot_general | solution.py:258
  115.2 3.0 %fusion.18 = f32[4,128,128]{2,1,0:T(8,128)S(1)} fusion(f32[4,1024,128]{2,1,0:T(8,128)} %fusion.60, pred[1024,128]{1,0:T(8,128)(4,1)S(1)} %copy-done.19, bf16[1024,4,128]{2,1,0:T(4,128)(2,1)} %reshape.350), kind=kOutput, calls=%fused_computation.33 | convolution fusion | flops 138412032 | bytes 3538944 | tf_op jit(solution)/shard_map/hrc,rhd->chd/dot_general | solution.py:259
  118.2 0.1 copy.121
  118.4 0.1 copy.123
  118.5 1.6 fusion.6.refs_0_
  120.2 0.7 broadcast_in_dim.75.refs_3_
  120.8 1.2 fusion.5
  122.1 0.1 copy.108
  122.2 0.8 copy.109
  122.9 2.2 %fusion.4 = bf16[64,1024]{1,0:T(8,128)(2,1)S(1)} fusion(bf16[8,128,64]{2,1,0:T(8,128)(2,1)} %get-tuple-element.20, bf16[8,128,1024]{2,1,0:T(8,128)(2,1)} %get-tuple-element.21), kind=kOutput, calls=%fused_computation.14 | convolution fusion | flops 134283264 | bytes 2359296 | tf_op jit(solution)/shard_map/dot_general | solution.py:248
  125.1 0.7 copy.163
  125.8 3.8 %fusion.87 = (f32[128]{0:T(128)S(1)}, f32[128]{0:T(128)S(1)}, f32[128,1024]{1,0:T(8,128)S(1)}) fusion(f32[128]{0:T(128)S(1)} %add_rsqrt_fusion.1, f32[128]{0:T(128)S(1)} %broadcast_multiply_fusion.5, bf16[1,128,1024]{2,1,0:T(8,128)(2,1)S(1)} %copy-done.1, bf16[128,2048]{1,0:T(8,128)(2,1)S(1)} %fusion.6.refs_0_, bf16[1024,2048]{1,0:T(8,128)(2,1)} %param.12), kind=kOutput, calls=%fused_computation.140 | convolution fusion | flops 537657088 | bytes 5507072 | tf_op jit(solution)/shard_map/dot_general | solution.py:280
  129.7 1.0 fusion.44
  130.6 31.5 %shard_map.130 = (bf16[8,128,2048]{2,1,0:T(8,128)(2,1)}, bf16[4,64,256]{2,1,0:T(8,128)(2,1)}, bf16[4,128,64]{2,1,0:T(8,128)(2,1)}, f32[4,8,256]{2,1,0:T(8,128)}) custom-call(bf16[128,2048]{1,0:T(8,128)(2,1)} %copy-done.2, bf16[4,64,256]{2,1,0:T(8,128)(2,1)} %bitcast.171, bf16[4,128,64]{2,1,0:T(8,128)(2,1)} %bitcast.170, f32[4,8,256]{2,1,0:T(8,128)} %broadcast_in_dim.75.refs_3_), custom_call_target="tpu_custom_call" | custom-call | tf_op jit(solution)/shard_map/pallas_call | solution.py:105
  162.2 2.9 %fusion = bf16[128,2048]{1,0:T(8,128)(2,1)S(1)} fusion(bf16[8,128,128]{2,1,0:T(8,128)(2,1)S(1)} %copy-done.15, bf16[8,128,2048]{2,1,0:T(8,128)(2,1)} %get-tuple-element.25), kind=kOutput, calls=%fused_computation.1 | convolution fusion | flops 537133056 | bytes 4980736 | tf_op jit(solution)/shard_map/dot_general | solution.py:278
  165.2 0.3 copy.111
  165.4 1.0 copy.112
  166.4 13.3 %shard_map.131 = bf16[4,128,512]{2,1,0:T(8,128)(2,1)} custom-call(bf16[4,128,512]{2,1,0:T(8,128)(2,1)} %bitcast.163), custom_call_target="tpu_custom_call" | custom-call | tf_op jit(solution)/shard_map/pallas_call | solution.py:105
  179.7 1.8 %convert_reduce_fusion = f32[128,512]{1,0:T(8,128)} fusion(bf16[4,128,512]{2,1,0:T(8,128)(2,1)} %shard_map.131), kind=kLoop, calls=%fused_computation.19 | loop fusion | flops 458752 | bytes 786432 | tf_op jit(solution)/shard_map/reduce_sum | solution.py:129
  181.6 0.6 slice.44
  182.1 0.6 convert_reduce_fusion.3
  182.8 0.7 copy.113
  (59 shorter events, 0.5 us)
Async XLA Ops:
  0.6 55.4 %copy-start = (bf16[512,1024]{1,0:T(8,128)(2,1)S(1)}, bf16[512,1024]{1,0:T(8,128)(2,1)}, u32[]{:S(2)}) copy-start(bf16[512,1024]{1,0:T(8,128)(2,1)} %param.13) | copy-start | bytes 3145732
  0.6 9.2 %copy-start.1 = (bf16[1,128,1024]{2,1,0:T(8,128)(2,1)S(1)}, bf16[1,128,1024]{2,1,0:T(8,128)(2,1)}, u32[]{:S(2)}) copy-start(bf16[1,128,1024]{2,1,0:T(8,128)(2,1)} %param.9) | copy-start | bytes 786436
  13.8 1.0 copy-start.4
  49.0 1.2 copy-start.8
  49.0 1.2 copy-start.20
  50.2 1.4 copy-start.7
  51.5 0.7 copy-start.10
  56.3 0.7 copy-start.11
  57.0 7.5 %copy-start.12 = (bf16[128,512]{0,1:T(8,128)(2,1)S(1)}, bf16[128,512]{0,1:T(8,128)(2,1)}, u32[]{:S(2)}) copy-start(bf16[128,512]{0,1:T(8,128)(2,1)} %copy.90) | copy-start | bytes 393220
  65.3 4.0 %copy-start.3 = (f32[128,512]{1,0:T(8,128)S(1)}, f32[128,512]{1,0:T(8,128)}, u32[]{:S(2)}) copy-start(f32[128,512]{1,0:T(8,128)} %copy.120) | copy-start | bytes 786436
  67.6 3.5 %copy-start.5 = (bf16[128,1024]{1,0:T(8,128)(2,1)}, bf16[128,1024]{1,0:T(8,128)(2,1)S(1)}, u32[]{:S(2)}) copy-start(bf16[128,1024]{1,0:T(8,128)(2,1)S(1)} %get-tuple-element.63.refs_1_) | copy-start | bytes 786436
  71.1 5.3 %copy-start.13 = (bf16[16,4,8,128]{3,2,1,0:T(8,128)(2,1)S(1)}, bf16[16,4,8,128]{3,2,1,0:T(8,128)(2,1)}, u32[]{:S(2)}) copy-start(bf16[16,4,8,128]{3,2,1,0:T(8,128)(2,1)} %get-tuple-element.53) | copy-start | bytes 393220
  78.2 32.9 %copy-start.19 = (pred[1024,128]{1,0:T(8,128)(4,1)S(1)}, pred[1024,128]{1,0:T(8,128)(4,1)}, u32[]{:S(2)}) copy-start(pred[1024,128]{1,0:T(8,128)(4,1)} %fusion.40) | copy-start | bytes 393220
  78.2 32.9 %copy-start.21 = (bf16[16,4,8,128]{3,2,1,0:T(8,128)(2,1)S(1)}, bf16[16,4,8,128]{3,2,1,0:T(8,128)(2,1)}, u32[]{:S(2)}) copy-start(bf16[16,4,8,128]{3,2,1,0:T(8,128)(2,1)} %get-tuple-element.52) | copy-start | bytes 393220
  115.2 3.2 %copy-start.16 = (f32[4,128,128]{2,1,0:T(8,128)S(1)}, f32[4,128,128]{2,1,0:T(8,128)}, u32[]{:S(2)}) copy-start(f32[4,128,128]{2,1,0:T(8,128)} %fusion.3) | copy-start | bytes 786436
  115.2 3.3 %copy-start.9 = (f32[128,512]{1,0:T(8,128)S(1)}, f32[128,512]{1,0:T(8,128)}, u32[]{:S(2)}) copy-start(f32[128,512]{1,0:T(8,128)} %get-tuple-element.50) | copy-start | bytes 786436
  118.2 1.9 %copy-start.22 = (f32[8,8,256]{2,1,0:T(8,128)S(1)}, f32[8,8,256]{2,1,0:T(8,128)}, u32[]{:S(2)}) copy-start(f32[8,8,256]{2,1,0:T(8,128)} %get-tuple-element.24) | copy-start | bytes 196612
  118.2 2.6 %copy-start.14 = (bf16[8,128,256]{2,1,0:T(8,128)(2,1)S(1)}, bf16[8,128,256]{2,1,0:T(8,128)(2,1)}, u32[]{:S(2)}) copy-start(bf16[8,128,256]{2,1,0:T(8,128)(2,1)} %get-tuple-element.23) | copy-start | bytes 1572868
  120.1 9.5 %copy-start.2 = (bf16[128,2048]{1,0:T(8,128)(2,1)}, bf16[128,2048]{1,0:T(8,128)(2,1)S(1)}, u32[]{:S(2)}) copy-start(bf16[128,2048]{1,0:T(8,128)(2,1)S(1)} %fusion.6.refs_0_) | copy-start | bytes 1572868
  125.8 3.9 %copy-start.6 = (f32[128,1024]{1,0:T(8,128)S(1)}, f32[128,1024]{1,0:T(8,128)}, u32[]{:S(2)}) copy-start(f32[128,1024]{1,0:T(8,128)} %get-tuple-element.64) | copy-start | bytes 1572868
  129.6 32.5 %copy-start.15 = (bf16[8,128,128]{2,1,0:T(8,128)(2,1)S(1)}, bf16[8,128,128]{2,1,0:T(8,128)(2,1)}, u32[]{:S(2)}) copy-start(bf16[8,128,128]{2,1,0:T(8,128)(2,1)} %get-tuple-element.19) | copy-start | bytes 786436
  165.1 16.4 %copy-start.23 = (f32[4,8,256]{2,1,0:T(8,128)S(1)}, f32[4,8,256]{2,1,0:T(8,128)}, u32[]{:S(2)}) copy-start(f32[4,8,256]{2,1,0:T(8,128)} %get-tuple-element.28) | copy-start | bytes 98308
  165.1 17.0 %copy-start.18 = (bf16[4,64,256]{2,1,0:T(8,128)(2,1)S(1)}, bf16[4,64,256]{2,1,0:T(8,128)(2,1)}, u32[]{:S(2)}) copy-start(bf16[4,64,256]{2,1,0:T(8,128)(2,1)} %get-tuple-element.26) | copy-start | bytes 393220
  165.2 17.6 %copy-start.17 = (bf16[4,128,64]{2,1,0:T(8,128)(2,1)S(1)}, bf16[4,128,64]{2,1,0:T(8,128)(2,1)}, u32[]{:S(2)}) copy-start(bf16[4,128,64]{2,1,0:T(8,128)(2,1)} %get-tuple-element.27) | copy-start | bytes 196612

commit v3 on v2

v3 whole, which is shorter than its diff:
```python
import functools

import jax
import jax.numpy as jnp
from jax import lax
from jax.experimental import pallas as pl
from jax.experimental.pallas import tpu as pltpu
from jax.sharding import PartitionSpec as P

HEADS = 4
DH = 128


NORM_EPS = 1e-05


def exchange_kernel(plan, *refs):
    count = len(plan)
    sources, targets = refs[:count], refs[count : 2 * count]
    send_sems, recv_sems, own_sems = refs[2 * count :]
    axes = sorted({axis for kind, axis in plan})
    barrier = pltpu.get_barrier_semaphore()
    for axis in axes:
        size, me = lax.axis_size(axis), lax.axis_index(axis)
        for step in range(1, size):
            pl.semaphore_signal(
                barrier,
                inc=1,
                device_id={axis: lax.rem(me + step, size)},
                device_id_type=pl.DeviceIdType.MESH,
            )
    pl.semaphore_wait(barrier, sum(lax.axis_size(axis) - 1 for axis in axes))

    def remote(source, target, number, slot, axis, peer):
        return pltpu.make_async_remote_copy(
            src_ref=source,
            dst_ref=target,
            send_sem=send_sems.at[number, slot],
            recv_sem=recv_sems.at[number, slot],
            device_id={axis: peer},
            device_id_type=pl.DeviceIdType.MESH,
        )

    sent, own, relays, landing = [], [], [], []
    for number, (kind, axis) in enumerate(plan):
        source, target = sources[number], targets[number]
        size, me = lax.axis_size(axis), lax.axis_index(axis)
        mine = source if kind == "gather" else source.at[me]
        own.append(pltpu.make_async_copy(mine, target.at[me], own_sems.at[number]))
        own[-1].start()
        if kind == "gather":
            sibling = me + 1 - 2 * lax.rem(me, 2)
            for step in range(1, size // 2):
                copy = remote(
                    source, target.at[me], number, step, axis, lax.rem(me + 2 * step, size)
                )
                copy.start()
                sent.append(copy)
                relays.append((number, axis, step, lax.rem(me + size - 2 * step, size), sibling))
            copy = remote(source, target.at[me], number, 0, axis, sibling)
            copy.start()
            sent.append(copy)
            landing.append(remote(source, target.at[sibling], number, 0, axis, sibling))
            for step in range(1, size // 2):
                origin = lax.rem(sibling + size - 2 * step, size)
                landing.append(
                    remote(source, target.at[origin], number, size // 2 + step, axis, sibling)
                )
        else:
            for step in range(1, size):
                peer = lax.rem(me + step, size)
                copy = remote(source.at[peer], target.at[me], number, step, axis, peer)
                copy.start()
                sent.append(copy)
                origin = lax.rem(me + size - step, size)
                landing.append(
                    remote(source.at[origin], target.at[origin], number, step, axis, origin)
                )
    for number, axis, step, origin, sibling in relays:
        size = lax.axis_size(axis)
        block = targets[number].at[origin]
        remote(sources[number], block, number, step, axis, origin).wait_recv()
        copy = remote(block, block, number, size // 2 + step, axis, sibling)
        copy.start()
        sent.append(copy)
    for copy in landing:
        copy.wait_recv()
    for copy in sent:
        copy.wait_send()
    for copy in own:
        copy.wait()


def exchange(identity, *items):
    plan = tuple((kind, axis) for kind, axis, array in items)
    arrays = [array for kind, axis, array in items]
    shapes = [
        jax.ShapeDtypeStruct(
            ((lax.axis_size(axis),) + array.shape) if kind == "gather" else array.shape,
            array.dtype,
        )
        for kind, axis, array in items
    ]
    slots = max(lax.axis_size(axis) for kind, axis in plan)
    return pl.pallas_call(
        functools.partial(exchange_kernel, plan),
        out_shape=shapes,
        in_specs=[pl.BlockSpec(memory_space=pl.ANY)] * len(arrays),
        out_specs=[pl.BlockSpec(memory_space=pl.ANY)] * len(arrays),
        scratch_shapes=[
            pltpu.SemaphoreType.DMA((len(arrays), slots)),
            pltpu.SemaphoreType.DMA((len(arrays), slots)),
            pltpu.SemaphoreType.DMA((len(arrays),)),
        ],
        compiler_params=pltpu.CompilerParams(collective_id=identity, has_side_effects=True),
    )(*arrays)


def blocks(array, count):
    rows, columns = array.shape
    return array.reshape(rows, count, columns // count).transpose(1, 0, 2)


def merged(array):
    return array.reshape(array.shape[0] * array.shape[1], array.shape[2])


def group_sum(array):
    return jnp.sum(array.astype(jnp.float32), axis=0)


def silu_slope(value):
    sigma = jax.nn.sigmoid(value)
    return sigma * (1.0 + value * (1.0 - sigma))


def norm_rows(value):
    centre = value - jnp.mean(value, axis=-1, keepdims=True)
    inverse = lax.rsqrt(jnp.mean(centre * centre, axis=-1, keepdims=True) + NORM_EPS)
    return (centre * inverse, inverse)


def norm_back(grad, normed, inverse):
    return inverse * (
        grad
        - jnp.mean(grad, axis=-1, keepdims=True)
        - normed * jnp.mean(grad * normed, axis=-1, keepdims=True)
    )


def marks(positions, lengths, targets):
    start = jnp.zeros_like(positions)
    first = jnp.zeros_like(positions)
    end = 0
    for number in range(lengths.shape[1]):
        length = lengths[0, number]
        begin, end = end, end + length
        inside = (positions >= begin) & (positions < end)
        start = jnp.where(inside, begin, start)
        first = jnp.where(inside, end - jnp.minimum(targets[0, number], length - 1), first)
    return start, positions >= first


def seen(query_pos, query_start, key_pos, key_tgt):
    same = (key_pos <= query_pos) & (key_pos >= query_start)
    return same & (jnp.logical_not(key_tgt) | (key_pos == query_pos))


def nt_dot(left, right):
    return lax.dot_general(
        left, right, (((1,), (1,)), ((), ())), preferred_element_type=jnp.float32
    )


def nn_dot(left, right):
    return jnp.dot(left, right, preferred_element_type=jnp.float32)


def store_blocks(target, value):
    width = target.shape[2]
    for number in range(target.shape[0]):
        target[number] = value[:, number * width : (number + 1) * width]


def head_cols(ref, column):
    part = ref[:, :, column : column + DH]
    return part.reshape(part.shape[0] * part.shape[1], DH)


def opening_kernel(x_ref, w_in_ref, normed_ref, pre_ref, gate_ref, rest_ref):
    normed, inverse = norm_rows(x_ref[...].astype(jnp.float32))
    normed_b = normed.astype(jnp.bfloat16)
    store_blocks(normed_ref, normed_b)
    width = gate_ref.shape[1]
    for number in range(4):
        columns = slice(number * width, (number + 1) * width)
        pre = nn_dot(normed_b, w_in_ref[:, columns])
        pre_ref[:, columns] = pre
        hidden_b = jax.nn.silu(pre).astype(jnp.bfloat16)
        if number == 0:
            gate_ref[...] = hidden_b
        else:
            rest_ref[:, (number - 1) * width : number * width] = hidden_b


def middle_kernel(
    divisor,
    lengths,
    targets,
    own_start,
    moved_ref,
    own_ref,
    gate_ref,
    pre_ref,
    x_ref,
    grad_ref,
    score_ref,
    head_score_ref,
    w_out_ref,
    w_score_ref,
    d_att_ref,
    d_total_ref,
    d_total_b_ref,
    d_mid_ref,
    head_ref,
    gated_ref,
    out_ref,
    d_pre_ref,
    attended_ref,
):
    rows, width = gate_ref.shape
    total = moved_ref.shape[0] * rows
    query_pos = own_start[0] + lax.broadcasted_iota(jnp.int32, (rows, 1), 0)
    key_pos = lax.broadcasted_iota(jnp.int32, (1, total), 1)
    query_start, query_tgt = marks(query_pos, lengths, targets)
    unused, key_tgt = marks(key_pos, lengths, targets)
    mask = seen(query_pos, query_start, key_pos, key_tgt)
    for head in range(HEADS):
        column = head * DH
        query = own_ref[:, width + column : width + column + DH]
        raw = nt_dot(query, head_cols(moved_ref, 2 * width + column)) * DH ** (-0.5)
        attn_b = jnp.where(mask, jax.nn.silu(raw) / divisor, 0.0).astype(jnp.bfloat16)
        attended_ref[:, column : column + DH] = nn_dot(attn_b, head_cols(moved_ref, column))
    onorm, att_inverse = norm_rows(attended_ref[...])
    gate_f = gate_ref[...].astype(jnp.float32)
    gated_b = (onorm * gate_f).astype(jnp.bfloat16)
    store_blocks(gated_ref, gated_b)
    output = x_ref[...].astype(jnp.float32) + nn_dot(gated_b, w_out_ref[...])
    out_b = output.astype(jnp.bfloat16)
    store_blocks(out_ref, out_b)
    mid_act = nn_dot(out_b, w_score_ref[...])
    weight_c = score_ref[...] * query_tgt.astype(jnp.float32)
    head_part = jnp.sum(weight_c * jax.nn.silu(mid_act), axis=0, keepdims=True)
    head_ref[...] = jnp.broadcast_to(head_part, head_ref.shape)
    d_mid_b = (weight_c * head_score_ref[...] * silu_slope(mid_act)).astype(jnp.bfloat16)
    d_mid_ref[...] = d_mid_b
    d_total = grad_ref[...].astype(jnp.float32) + nt_dot(d_mid_b, w_score_ref[...])
    d_total_ref[...] = d_total
    d_total_b = d_total.astype(jnp.bfloat16)
    d_total_b_ref[...] = d_total_b
    d_gated = nt_dot(d_total_b, w_out_ref[...])
    d_pre_ref[...] = (d_gated * onorm * silu_slope(pre_ref[:, 0:width])).astype(jnp.bfloat16)
    d_att_ref[...] = norm_back(d_gated * gate_f, onorm, att_inverse).astype(jnp.bfloat16)


def closing_kernel(
    divisor,
    lengths,
    targets,
    own_start,
    moved_ref,
    grad_all_ref,
    own_ref,
    own_grad_ref,
    pre_ref,
    d_pre_gate_ref,
    x_ref,
    d_total_ref,
    w_in_ref,
    d_pre_ref,
    d_x_ref,
):
    rows, width = own_grad_ref.shape
    total = moved_ref.shape[0] * rows
    own_col = own_start[0] + lax.broadcasted_iota(jnp.int32, (rows, 1), 0)
    all_row = lax.broadcasted_iota(jnp.int32, (1, total), 1)
    own_first, own_tgt = marks(own_col, lengths, targets)
    all_first, all_tgt = marks(all_row, lengths, targets)
    mask = seen(own_col, own_first, all_row, all_tgt)
    key_mask = seen(all_row, all_first, own_col, own_tgt)
    scale = DH ** (-0.5)

    def store(kind, column, value):
        columns = slice(kind * width + column, kind * width + column + DH)
        slope = silu_slope(pre_ref[:, columns])
        d_pre_ref[:, columns] = (value * slope).astype(jnp.bfloat16)

    d_pre_ref[:, 0:width] = d_pre_gate_ref[...]
    for head in range(HEADS):
        column = head * DH
        value_own = own_ref[:, column : column + DH]
        query_own = own_ref[:, width + column : width + column + DH]
        key_own = own_ref[:, 2 * width + column : 2 * width + column + DH]
        grad_own = own_grad_ref[:, column : column + DH]
        value_all = head_cols(moved_ref, column)
        query_all = head_cols(moved_ref, width + column)
        key_all = head_cols(moved_ref, 2 * width + column)
        grad_all = head_cols(grad_all_ref, column)
        raw = nt_dot(query_own, key_all) * scale
        factor = jnp.where(mask, silu_slope(raw) * scale / divisor, 0.0)
        d_raw_b = (nt_dot(grad_own, value_all) * factor).astype(jnp.bfloat16)
        store(2, column, nn_dot(d_raw_b, key_all))
        raw = nt_dot(key_own, query_all) * scale
        sigma = jax.nn.sigmoid(raw)
        attn_b = jnp.where(key_mask, raw * sigma / divisor, 0.0).astype(jnp.bfloat16)
        slope = sigma * (1.0 + raw * (1.0 - sigma))
        factor = jnp.where(key_mask, slope * scale / divisor, 0.0)
        d_raw_b = (nt_dot(value_own, grad_all) * factor).astype(jnp.bfloat16)
        store(3, column, nn_dot(d_raw_b, query_all))
        store(1, column, nn_dot(attn_b, grad_all))
    normed, inverse = norm_rows(x_ref[...].astype(jnp.float32))
    d_normed = nt_dot(d_pre_ref[...], w_in_ref[...])
    d_x = d_total_ref[...] + norm_back(d_normed, normed, inverse)
    d_x_ref[...] = d_x.astype(jnp.bfloat16)


def local_call(kernel, scalars, arrays, outs, scratch=()):
    return pl.pallas_call(
        kernel,
        out_shape=[jax.ShapeDtypeStruct(shape, kind) for shape, kind in outs],
        in_specs=[pl.BlockSpec(memory_space=pltpu.SMEM)] * len(scalars)
        + [pl.BlockSpec(memory_space=pltpu.VMEM)] * len(arrays),
        out_specs=[pl.BlockSpec(memory_space=pltpu.VMEM)] * len(outs),
        scratch_shapes=list(scratch),
        compiler_params=pltpu.CompilerParams(vmem_limit_bytes=56 * 1024 * 1024),
    )(*scalars, *arrays)


def on_device(x_rows, lengths, targets, w_in, w_out, w_score, head_score, grad_out, grad_score):
    rows, features = x_rows.shape[1:]
    seq_count = lax.axis_size("seq")
    group_count = lax.axis_size("dp")
    total = rows * seq_count
    width = w_out.shape[0]
    middle = head_score.shape[0]
    divisor = float(total // 2)
    half, full = jnp.bfloat16, jnp.float32
    own_start = (lax.axis_index("seq") * rows).astype(jnp.int32)[None]
    scalars = (lengths, targets, own_start)
    normed_blocks, pre_act, gate_b, own_b = local_call(
        opening_kernel,
        (),
        (x_rows[0], w_in),
        (
            ((seq_count, rows, features // seq_count), half),
            ((rows, 4 * width), full),
            ((rows, width), half),
            ((rows, 3 * width), half),
        ),
    )
    moved, normed_cols = exchange(
        1, ("gather", "seq", own_b), ("swap", "seq", normed_blocks)
    )
    d_att_b, d_total, d_total_b, d_mid_b, head_part, gated_blocks, out_blocks, d_pre_gate = (
        local_call(
            functools.partial(middle_kernel, divisor),
            scalars,
            (
                moved,
                own_b,
                gate_b,
                pre_act,
                x_rows[0],
                grad_out[0],
                grad_score[0][:, None],
                head_score[None, :],
                w_out,
                w_score,
            ),
            (
                ((rows, width), half),
                ((rows, features), full),
                ((rows, features), half),
                ((rows, middle), half),
                ((8, middle), full),
                ((seq_count, rows, width // seq_count), half),
                ((seq_count, rows, features // seq_count), half),
                ((rows, width), half),
            ),
            (pltpu.VMEM((rows, width), full),),
        )
    )
    grad_all, total_all, mid_all, head_all, gated_cols, out_cols = exchange(
        2,
        ("gather", "seq", d_att_b),
        ("gather", "seq", d_total_b),
        ("gather", "seq", d_mid_b),
        ("gather", "seq", head_part),
        ("swap", "seq", gated_blocks),
        ("swap", "seq", out_blocks),
    )
    out_part = nn_dot(merged(gated_cols).T, merged(total_all))
    score_part = nn_dot(merged(out_cols).T, merged(mid_all))
    head_group = jnp.sum(head_all, axis=0)
    d_pre_b, d_x = local_call(
        functools.partial(closing_kernel, divisor),
        scalars,
        (moved, grad_all, own_b, d_att_b, pre_act, d_pre_gate, x_rows[0], d_total, w_in),
        (((rows, 4 * width), half), ((rows, features), half)),
    )
    pre_all, out_parts, score_parts, head_parts = exchange(
        3,
        ("gather", "seq", d_pre_b),
        ("swap", "dp", blocks(out_part.astype(half), group_count)),
        ("swap", "dp", blocks(score_part.astype(half), group_count)),
        ("swap", "dp", jnp.broadcast_to(head_group, (group_count,) + head_group.shape)),
    )
    in_part = nn_dot(merged(normed_cols).T, merged(pre_all))
    (in_parts,) = exchange(4, ("swap", "dp", blocks(in_part.astype(half), group_count)))
    return (
        d_x[None],
        group_sum(in_parts),
        group_sum(out_parts),
        group_sum(score_parts),
        group_sum(head_parts)[0],
    )


def solution(mesh):
    placed = (
        P("dp", "seq", None),
        P("dp", None),
        P("dp", None),
        P(),
        P(),
        P(),
        P(),
        P("dp", "seq", None),
        P("dp", "seq"),
    )
    return jax.shard_map(
        on_device,
        mesh=mesh,
        in_specs=placed,
        out_specs=(P("dp", "seq", None), P("seq", "dp"), P("seq", "dp"), P("seq", "dp"), P()),
        check_vma=False,
    )
```

time: 184 us -> 137 us (0.74)
  matrix products: 35.5 us -> 3.74 us
  local copies, waits for them, and re-layouts: 28.7 us -> 6.13 us
  Pallas kernels: 101 us -> 123 us
  other arithmetic: 17.1 us -> 2.53 us
    dot_general x15 -> x3, matrix products: 35.5 us -> 3.74 us  [nn_dot(): return jnp.dot(left, right, preferred_element_type=jnp.float32)]
    pallas_call x0 -> x3, Pallas kernels: none -> 22 us  [local_call(): pl.pallas_call(kernel, out_shape=[jax.ShapeDtypeStruct(shape, kind) for s...]
    slice x3 -> x0, local copies, waits for them, and re-layouts: 6.51 us -> none  [the longest x2 5.71 us: on_device(): moved[:, at * width:(at + 1) * width].reshape(total, HEADS, DH)]
    unnamed x53 -> x19, local copies, waits for them, and re-layouts: 6.38 us -> 0.74 us
    reshape x5 -> x0, local copies, waits for them, and re-layouts: 5.3 us -> none  [the longest x1 2.18 us: on_device(): grad_all = grad_all.reshape(total, HEADS, DH)]
    mul x2 -> x0, other arithmetic: 2.93 us -> none  [the longest x1 1.76 us: on_device(): d_gate = d_gated * onorm]
    convert_element_type x2 -> x0, other arithmetic: 2.69 us -> none  [the longest x1 1.59 us: on_device(): d_pre_b = (d_hidden * silu_slope(pre_act)).astype(jnp.bfloat16)]
    reshape x5 -> x3, local copies, waits for them, and re-layouts: 5.1 us -> 2.44 us  [blocks(): return array.reshape(rows, count, columns // count).transpose(1, 0, 2)]
where the time goes in v3:
time: 137 us; the launch traced here: 136 us
  Pallas kernels  123 us (90%)
  local copies, waits for them, and re-layouts  6.13 us (4%)
  matrix products  3.74 us (3%)
  other arithmetic  2.53 us (2%)
    pallas_call x4, Pallas kernels, exchange(): pl.pallas_call(functools.partial(exchange_kernel, plan), out_shape=shapes...  101 us
    pallas_call x3, Pallas kernels, local_call(): pl.pallas_call(kernel, out_shape=[jax.ShapeDtypeStruct(shape, kind) for s...  22 us
    dot_general x3, matrix products, nn_dot(): return jnp.dot(left, right, preferred_element_type=jnp.float32)  3.74 us

profile of v3, /device:TPU:0, one launch (start us, length us, event | category | flops | bytes accessed | tf_op | source)
XLA Modules:
  0.0 136.3 jit_solution(11216605102098513052)
XLA Ops:
  0.6 1.4 %copy.27.score_ref = f32[128,1]{1,0:T(8,128)} copy(f32[128,1]{0,1:T(1,128)} %bitcast.48) | data formatting | bytes 1024 | tf_op jit(solution)/shard_map/broadcast_in_dim;squeeze | solution.py:375
  2.0 4.4 %shard_map.128 = (bf16[8,128,128]{2,1,0:T(8,128)(2,1)}, f32[128,2048]{1,0:T(8,128)}, bf16[128,512]{1,0:T(8,128)(2,1)}, bf16[128,1536]{1,0:T(8,128)(2,1)}) custom-call(bf16[128,1024]{1,0:T(8,128)(2,1)} %bitcast.36, bf16[1024,2048]{1,0:T(8,128)(2,1)} %w_in_ref.3), custom_call_target="tpu_custom_call" | custom-call | tf_op jit(solution)/shard_map/pallas_call | solution.py:328
  6.4 25.7 %shard_map.129 = (bf16[8,128,1536]{2,1,0:T(8,128)(2,1)}, bf16[8,128,128]{2,1,0:T(8,128)(2,1)}) custom-call(bf16[128,1536]{1,0:T(8,128)(2,1)} %get-tuple-element.31.refs_0_.own_ref, bf16[8,128,128]{2,1,0:T(8,128)(2,1)} %get-tuple-element.32.refs_1_), custom_call_target="tpu_custom_call" | custom-call | tf_op jit(solution)/shard_map/pallas_call | solution.py:105
  32.1 6.5 %shard_map.130 = (bf16[128,512]{1,0:T(8,128)(2,1)}, f32[128,1024]{1,0:T(8,128)}, bf16[128,1024]{1,0:T(8,128)(2,1)}, bf16[128,256]{1,0:T(8,128)(2,1)}, f32[8,256]...) custom-call(s32[1,8]{1,0:T(1,128)} %lengths.3, ...), custom_call_target="tpu_custom_call" | custom-call | tf_op jit(solution)/shard_map/pallas_call | solution.py:328
  38.7 30.7 %shard_map.131 = (bf16[8,128,512]{2,1,0:T(8,128)(2,1)}, bf16[8,128,1024]{2,1,0:T(8,128)(2,1)}, bf16[8,128,256]{2,1,0:T(8,128)(2,1)}, f32[8,8,256]{2,1,0:T(8,128)...) custom-call(bf16[128,512]{1,0:T(8,128)(2,1)} %get-tuple-element.36.refs_0_.own_grad_ref, ...), custom_call_target="tpu_custom_call" | custom-call | tf_op jit(solution)/shard_map/pallas_call | solution.py:105
  69.4 0.0 copy-start.7
  69.4 0.0 copy-start.1
  69.4 0.0 copy-start.4
  69.4 0.0 copy-start
  69.4 0.0 copy-start.3
  69.4 11.0 %shard_map.132 = (bf16[128,2048]{1,0:T(8,128)(2,1)}, bf16[128,1024]{1,0:T(8,128)(2,1)}) custom-call(s32[1,8]{1,0:T(1,128)} %lengths.3, s32[1,8]{1,0:T(1,128)} %targets.3, s32[1]{0:T(128)} %bitcast.own_start, bf16[8,128,1536]{2,1,0:T(8,128)(2,1)} %get-tuple-element.33.moved_ref, bf16[8,128,512]{2,1,0:T(8,128)(2,1)} %get-tuple-element.42.grad_all_ref, ...), custom_call_target="tpu_custom_call" | custom-call | tf_op jit(solution)/shard_map/pallas_call | solution.py:328
  80.4 0.0 copy-start.2
  80.4 0.0 copy-done.7
  80.5 0.6 broadcast_in_dim.15.refs_3_
  81.1 0.0 copy-done.1
  81.1 0.0 copy-done.4
  81.1 0.3 fusion.2
  81.4 0.1 copy.31
  81.5 0.8 copy.32
  82.2 0.0 copy-done
  82.2 0.0 copy-done.3
  82.3 0.5 fusion.1
  82.8 0.7 copy.42
  83.4 31.5 %shard_map.133 = (bf16[8,128,2048]{2,1,0:T(8,128)(2,1)}, bf16[4,64,256]{2,1,0:T(8,128)(2,1)}, bf16[4,128,64]{2,1,0:T(8,128)(2,1)}, f32[4,8,256]{2,1,0:T(8,128)}) custom-call(bf16[128,2048]{1,0:T(8,128)(2,1)} %get-tuple-element.47.refs_0_, bf16[4,64,256]{2,1,0:T(8,128)(2,1)} %bitcast.42, bf16[4,128,64]{2,1,0:T(8,128)(2,1)} %bitcast.41, ...), custom_call_target="tpu_custom_call" | custom-call | tf_op jit(solution)/shard_map/pallas_call | solution.py:105
  115.0 0.0 copy-done.2
  115.0 0.0 copy-start.8
  115.0 0.0 copy-start.6
  115.0 0.0 copy-start.5
  115.0 3.0 %fusion = bf16[128,2048]{1,0:T(8,128)(2,1)S(1)} fusion(bf16[8,128,128]{2,1,0:T(8,128)(2,1)S(1)} %copy-done.2, bf16[8,128,2048]{2,1,0:T(8,128)(2,1)} %get-tuple-element.53), kind=kOutput, calls=%fused_computation.1 | convolution fusion | flops 537133056 | bytes 4980736 | tf_op jit(solution)/shard_map/dot_general | solution.py:176
  118.0 0.3 copy.34
  118.2 1.0 copy.35
  119.2 13.3 %shard_map.134 = bf16[4,128,512]{2,1,0:T(8,128)(2,1)} custom-call(bf16[4,128,512]{2,1,0:T(8,128)(2,1)} %bitcast.40), custom_call_target="tpu_custom_call" | custom-call | tf_op jit(solution)/shard_map/pallas_call | solution.py:105
  132.5 1.8 %convert_reduce_fusion = f32[128,512]{1,0:T(8,128)} fusion(bf16[4,128,512]{2,1,0:T(8,128)(2,1)} %shard_map.134), kind=kLoop, calls=%fused_computation.6 | loop fusion | flops 458752 | bytes 786432 | tf_op jit(solution)/shard_map/reduce_sum | solution.py:129
  134.4 0.0 copy-done.8
  134.4 0.6 slice.4
  134.9 0.0 copy-done.6
  134.9 0.6 convert_reduce_fusion.2
  135.6 0.0 copy-done.5
  135.6 0.7 copy.36
  (3 shorter events, 0.0 us)
Async XLA Ops:
  69.4 11.1 %copy-start.7 = (f32[8,8,256]{2,1,0:T(8,128)S(1)}, f32[8,8,256]{2,1,0:T(8,128)}, u32[]{:S(2)}) copy-start(f32[8,8,256]{2,1,0:T(8,128)} %get-tuple-element.52) | copy-start | bytes 196612
  69.4 11.7 %copy-start.1 = (bf16[8,128,256]{2,1,0:T(8,128)(2,1)S(1)}, bf16[8,128,256]{2,1,0:T(8,128)(2,1)}, u32[]{:S(2)}) copy-start(bf16[8,128,256]{2,1,0:T(8,128)(2,1)} %get-tuple-element.51) | copy-start | bytes 1572868
  69.4 11.7 %copy-start.4 = (bf16[8,128,128]{2,1,0:T(8,128)(2,1)S(1)}, bf16[8,128,128]{2,1,0:T(8,128)(2,1)}, u32[]{:S(2)}) copy-start(bf16[8,128,128]{2,1,0:T(8,128)(2,1)} %get-tuple-element.50) | copy-start | bytes 786436
  69.4 12.8 %copy-start = (bf16[8,128,1024]{2,1,0:T(8,128)(2,1)S(1)}, bf16[8,128,1024]{2,1,0:T(8,128)(2,1)}, u32[]{:S(2)}) copy-start(bf16[8,128,1024]{2,1,0:T(8,128)(2,1)} %get-tuple-element.49) | copy-start | bytes 6291460
  69.4 12.8 %copy-start.3 = (bf16[8,128,64]{2,1,0:T(8,128)(2,1)S(1)}, bf16[8,128,64]{2,1,0:T(8,128)(2,1)}, u32[]{:S(2)}) copy-start(bf16[8,128,64]{2,1,0:T(8,128)(2,1)} %get-tuple-element.48) | copy-start | bytes 393220
  80.4 34.5 %copy-start.2 = (bf16[8,128,128]{2,1,0:T(8,128)(2,1)S(1)}, bf16[8,128,128]{2,1,0:T(8,128)(2,1)}, u32[]{:S(2)}) copy-start(bf16[8,128,128]{2,1,0:T(8,128)(2,1)} %get-tuple-element.46) | copy-start | bytes 786436
  115.0 19.4 %copy-start.8 = (f32[4,8,256]{2,1,0:T(8,128)S(1)}, f32[4,8,256]{2,1,0:T(8,128)}, u32[]{:S(2)}) copy-start(f32[4,8,256]{2,1,0:T(8,128)} %get-tuple-element.56) | copy-start | bytes 98308
  115.0 20.0 %copy-start.6 = (bf16[4,64,256]{2,1,0:T(8,128)(2,1)S(1)}, bf16[4,64,256]{2,1,0:T(8,128)(2,1)}, u32[]{:S(2)}) copy-start(bf16[4,64,256]{2,1,0:T(8,128)(2,1)} %get-tuple-element.54) | copy-start | bytes 393220
  115.0 20.6 %copy-start.5 = (bf16[4,128,64]{2,1,0:T(8,128)(2,1)S(1)}, bf16[4,128,64]{2,1,0:T(8,128)(2,1)}, u32[]{:S(2)}) copy-start(bf16[4,128,64]{2,1,0:T(8,128)(2,1)} %get-tuple-element.55) | copy-start | bytes 196612

commit v4 on v3

--- a/solution.py
+++ b/solution.py
@@ -220,12 +220,10 @@
     w_score_ref,
     d_att_ref,
     d_total_ref,
-    d_total_b_ref,
-    d_mid_ref,
+    early_ref,
     head_ref,
     gated_ref,
     out_ref,
-    d_pre_ref,
     attended_ref,
 ):
     rows, width = gate_ref.shape
@@ -253,13 +251,15 @@
     head_part = jnp.sum(weight_c * jax.nn.silu(mid_act), axis=0, keepdims=True)
     head_ref[...] = jnp.broadcast_to(head_part, head_ref.shape)
     d_mid_b = (weight_c * head_score_ref[...] * silu_slope(mid_act)).astype(jnp.bfloat16)
-    d_mid_ref[...] = d_mid_b
+    features, middle = x_ref.shape[1], d_mid_b.shape[1]
+    early_ref[:, features : features + middle] = d_mid_b
     d_total = grad_ref[...].astype(jnp.float32) + nt_dot(d_mid_b, w_score_ref[...])
     d_total_ref[...] = d_total
     d_total_b = d_total.astype(jnp.bfloat16)
-    d_total_b_ref[...] = d_total_b
+    early_ref[:, 0:features] = d_total_b
     d_gated = nt_dot(d_total_b, w_out_ref[...])
-    d_pre_ref[...] = (d_gated * onorm * silu_slope(pre_ref[:, 0:width])).astype(jnp.bfloat16)
+    d_pre_gate = d_gated * onorm * silu_slope(pre_ref[:, 0:width])
+    early_ref[:, features + middle :] = d_pre_gate.astype(jnp.bfloat16)
     d_att_ref[...] = norm_back(d_gated * gate_f, onorm, att_inverse).astype(jnp.bfloat16)
 
 
@@ -273,7 +273,7 @@
     own_ref,
     own_grad_ref,
     pre_ref,
-    d_pre_gate_ref,
+    early_ref,
     x_ref,
     d_total_ref,
     w_in_ref,
@@ -291,11 +291,10 @@
     scale = DH ** (-0.5)
 
     def store(kind, column, value):
-        columns = slice(kind * width + column, kind * width + column + DH)
-        slope = silu_slope(pre_ref[:, columns])
-        d_pre_ref[:, columns] = (value * slope).astype(jnp.bfloat16)
-
-    d_pre_ref[:, 0:width] = d_pre_gate_ref[...]
+        first = kind * width + column
+        slope = silu_slope(pre_ref[:, first : first + DH])
+        d_pre_ref[:, first - width : first - width + DH] = (value * slope).astype(jnp.bfloat16)
+
     for head in range(HEADS):
         column = head * DH
         value_own = own_ref[:, column : column + DH]
@@ -319,7 +318,9 @@
         store(3, column, nn_dot(d_raw_b, query_all))
         store(1, column, nn_dot(attn_b, grad_all))
     normed, inverse = norm_rows(x_ref[...].astype(jnp.float32))
-    d_normed = nt_dot(d_pre_ref[...], w_in_ref[...])
+    gate_at = early_ref.shape[1] - width
+    d_normed = nt_dot(early_ref[:, gate_at:], w_in_ref[:, 0:width])
+    d_normed = d_normed + nt_dot(d_pre_ref[...], w_in_ref[:, width:])
     d_x = d_total_ref[...] + norm_back(d_normed, normed, inverse)
     d_x_ref[...] = d_x.astype(jnp.bfloat16)
 
@@ -361,7 +362,7 @@
     moved, normed_cols = exchange(
         1, ("gather", "seq", own_b), ("swap", "seq", normed_blocks)
     )
-    d_att_b, d_total, d_total_b, d_mid_b, head_part, gated_blocks, out_blocks, d_pre_gate = (
+    d_att_b, d_total, early_b, head_part, gated_blocks, out_blocks = (
         local_call(
             functools.partial(middle_kernel, divisor),
             scalars,
@@ -380,43 +381,45 @@
             (
                 ((rows, width), half),
                 ((rows, features), full),
-                ((rows, features), half),
-                ((rows, middle), half),
+                ((rows, features + middle + width), half),
                 ((8, middle), full),
                 ((seq_count, rows, width // seq_count), half),
                 ((seq_count, rows, features // seq_count), half),
-                ((rows, width), half),
             ),
             (pltpu.VMEM((rows, width), full),),
         )
     )
-    grad_all, total_all, mid_all, head_all, gated_cols, out_cols = exchange(
-        2,
-        ("gather", "seq", d_att_b),
-        ("gather", "seq", d_total_b),
-        ("gather", "seq", d_mid_b),
-        ("gather", "seq", head_part),
+    early_all = lax.all_gather(early_b, "seq", axis=0, tiled=True)
+    grad_all, head_all = exchange(
+        2, ("gather", "seq", d_att_b), ("gather", "seq", head_part)
+    )
+    d_rest_b, d_x = local_call(
+        functools.partial(closing_kernel, divisor),
+        scalars,
+        (moved, grad_all, own_b, d_att_b, pre_act, early_b, x_rows[0], d_total, w_in),
+        (((rows, 3 * width), half), ((rows, features), half)),
+    )
+    rest_all, gated_cols, out_cols = exchange(
+        3,
+        ("gather", "seq", d_rest_b),
         ("swap", "seq", gated_blocks),
         ("swap", "seq", out_blocks),
     )
-    out_part = nn_dot(merged(gated_cols).T, merged(total_all))
-    score_part = nn_dot(merged(out_cols).T, merged(mid_all))
+    out_part = nn_dot(merged(gated_cols).T, early_all[:, 0:features])
+    score_part = nn_dot(merged(out_cols).T, early_all[:, features : features + middle])
+    normed_t = merged(normed_cols).T
+    in_part = jnp.concatenate(
+        [nn_dot(normed_t, early_all[:, features + middle :]), nn_dot(normed_t, merged(rest_all))],
+        axis=1,
+    )
     head_group = jnp.sum(head_all, axis=0)
-    d_pre_b, d_x = local_call(
-        functools.partial(closing_kernel, divisor),
-        scalars,
-        (moved, grad_all, own_b, d_att_b, pre_act, d_pre_gate, x_rows[0], d_total, w_in),
-        (((rows, 4 * width), half), ((rows, features), half)),
-    )
-    pre_all, out_parts, score_parts, head_parts = exchange(
-        3,
-        ("gather", "seq", d_pre_b),
+    in_parts, out_parts, score_parts, head_parts = exchange(
+        4,
+        ("swap", "dp", blocks(in_part.astype(half), group_count)),
         ("swap", "dp", blocks(out_part.astype(half), group_count)),
         ("swap", "dp", blocks(score_part.astype(half), group_count)),
         ("swap", "dp", jnp.broadcast_to(head_group, (group_count,) + head_group.shape)),
     )
-    in_part = nn_dot(merged(normed_cols).T, merged(pre_all))
-    (in_parts,) = exchange(4, ("swap", "dp", blocks(in_part.astype(half), group_count)))
     return (
         d_x[None],
         group_sum(in_parts),

time: 137 us -> 149 us (1.088)
  between operations: 0.8 us -> 14.2 us
  Pallas kernels: 123 us -> 116 us
  matrix products: 3.74 us -> 7.53 us
  other arithmetic: 2.53 us -> 5.15 us
    pallas_call x4, Pallas kernels: 101 us -> 94.2 us  [exchange(): pl.pallas_call(functools.partial(exchange_kernel, plan), out_shape=shapes...]
    dot_general x3 -> x4, matrix products: 3.74 us -> 7.53 us  [nn_dot(): return jnp.dot(left, right, preferred_element_type=jnp.float32)]
    reduce_sum x4, other arithmetic: 2.52 us -> 5.1 us  [group_sum(): return jnp.sum(array.astype(jnp.float32), axis=0)]
  transfers between devices with their start and end apart: 0 -> 1, of which waited for: 0 -> 0; matrix products, arithmetic and copies ran while one was open for 0% -> 2% of each run, Pallas kernels for 0% -> 38%
where the time goes in v4:
time: 149 us
  Pallas kernels  116 us (78%)
  between operations  14.2 us (10%)
  matrix products  7.53 us (5%)
  local copies, waits for them, and re-layouts  6.14 us (4%)
  other arithmetic  5.15 us (3%)
    pallas_call x4, Pallas kernels, exchange(): pl.pallas_call(functools.partial(exchange_kernel, plan), out_shape=shapes...  94.2 us
    pallas_call x3, Pallas kernels, local_call(): pl.pallas_call(kernel, out_shape=[jax.ShapeDtypeStruct(shape, kind) for s...  21.8 us
    dot_general x4, matrix products, nn_dot(): return jnp.dot(left, right, preferred_element_type=jnp.float32)  7.53 us
    reduce_sum x4, other arithmetic, group_sum(): return jnp.sum(array.astype(jnp.float32), axis=0)  5.1 us
  transfers between devices with their start and end apart: 1, of which 0 were waited for; matrix products, arithmetic and copies ran while one was open for 2% of the time, Pallas kernels for 38%

profile of v4, /device:TPU:0, one launch (start us, length us, event | category | flops | bytes accessed | tf_op | source)
XLA Modules:
  0.0 149.1 jit_solution(15954852846771412865)
XLA Ops:
  7.2 0.0 all-gather.2.cloned.1.call-start
  7.2 1.4 copy.23.score_ref
  8.6 4.3 %shard_map.128 = (bf16[8,128,128]{2,1,0:T(8,128)(2,1)}, f32[128,2048]{1,0:T(8,128)}, bf16[128,512]{1,0:T(8,128)(2,1)}, bf16[128,1536]{1,0:T(8,128)(2,1)}) custom-call(bf16[128,1024]{1,0:T(8,128)(2,1)} %bitcast.30, bf16[1024,2048]{1,0:T(8,128)(2,1)} %w_in_ref.3), custom_call_target="tpu_custom_call" | custom-call | tf_op jit(solution)/shard_map/pallas_call | solution.py:329
  12.9 25.7 %shard_map.129 = (bf16[8,128,1536]{2,1,0:T(8,128)(2,1)}, bf16[8,128,128]{2,1,0:T(8,128)(2,1)}) custom-call(bf16[128,1536]{1,0:T(8,128)(2,1)} %get-tuple-element.28.refs_0_.own_ref, bf16[8,128,128]{2,1,0:T(8,128)(2,1)} %get-tuple-element.29.refs_1_), custom_call_target="tpu_custom_call" | custom-call | tf_op jit(solution)/shard_map/pallas_call | solution.py:105
  38.6 6.5 %shard_map.130 = (bf16[128,512]{1,0:T(8,128)(2,1)}, f32[128,1024]{1,0:T(8,128)}, bf16[128,1792]{1,0:T(8,128)(2,1)}, f32[8,256]{1,0:T(8,128)}, bf16[8,128,64]{2,1,0:T(8,128)(2,1)}, /*index=5*/bf16[8,128,128]{2,1,0:T(8,128)(2,1)}) custom-call(s32[1,8]{1,0:T(1,128)} %lengths.3, s32[1,8]{1,0:T(1,128)} %targets.3, s32[1]{0:T(128)} %bitcast.own_start, ...), custom_call_target="tpu_custom_call" | custom-call | tf_op jit(solution)/shard_map/pallas_call | solution.py:329
  45.1 0.0 all-gather.2.cloned.1.call-update
  45.2 11.9 %shard_map.131 = (bf16[8,128,512]{2,1,0:T(8,128)(2,1)}, f32[8,8,256]{2,1,0:T(8,128)}) custom-call(bf16[128,512]{1,0:T(8,128)(2,1)} %get-tuple-element.33.refs_0_.own_grad_ref, f32[8,256]{1,0:T(8,128)} %get-tuple-element.34.refs_1_), custom_call_target="tpu_custom_call" | custom-call | tf_op jit(solution)/shard_map/pallas_call | solution.py:105
  57.0 0.0 copy-start.3
  57.0 0.0 copy-start
  57.0 11.0 %shard_map.132 = (bf16[128,1536]{1,0:T(8,128)(2,1)}, bf16[128,1024]{1,0:T(8,128)(2,1)}) custom-call(s32[1,8]{1,0:T(1,128)} %lengths.3, s32[1,8]{1,0:T(1,128)} %targets.3, s32[1]{0:T(128)} %bitcast.own_start, bf16[8,128,1536]{2,1,0:T(8,128)(2,1)} %get-tuple-element.30.moved_ref, bf16[8,128,512]{2,1,0:T(8,128)(2,1)} %get-tuple-element.35.grad_all_ref, ...), custom_call_target="tpu_custom_call" | custom-call | tf_op jit(solution)/shard_map/pallas_call | solution.py:329
  68.0 0.0 copy-done.3
  68.0 33.7 %shard_map.133 = (bf16[8,128,1536]{2,1,0:T(8,128)(2,1)}, bf16[8,128,64]{2,1,0:T(8,128)(2,1)}, bf16[8,128,128]{2,1,0:T(8,128)(2,1)}) custom-call(bf16[128,1536]{1,0:T(8,128)(2,1)} %get-tuple-element.40.refs_0_, bf16[8,128,64]{2,1,0:T(8,128)(2,1)} %get-tuple-element.41.refs_1_, bf16[8,128,128]{2,1,0:T(8,128)(2,1)} %get-tuple-element.42.refs_2_), custom_call_target="tpu_custom_call" | custom-call | tf_op jit(solution)/shard_map/pallas_call | solution.py:105
  101.7 0.0 copy-done
  101.7 0.0 copy-start.1
  101.8 2.5 %fusion = bf16[128,1536]{1,0:T(8,128)(2,1)S(1)} fusion(bf16[8,128,128]{2,1,0:T(8,128)(2,1)S(1)} %copy-done, bf16[8,128,1536]{2,1,0:T(8,128)(2,1)} %get-tuple-element.43), kind=kOutput, calls=%fused_computation.1 | convolution fusion | flops 402849792 | bytes 3801088 | tf_op jit(solution)/shard_map/dot_general | solution.py:176
  104.3 0.0 all-gather.2.cloned.1.call-done
  104.3 0.0 copy-start.2
  104.3 1.6 %convolution_convert_fusion = bf16[128,512]{1,0:T(8,128)(2,1)S(1)} fusion(bf16[1024,128]{1,0:T(8,128)(2,1)S(1)} %bitcast.35, bf16[1024,1792]{1,0:T(8,128)(2,1)} %all-gather.2.cloned.1.call-done), kind=kOutput, calls=%fused_computation.5 | convolution fusion | flops 134283264 | bytes 1441792 | tf_op jit(solution)/shard_map/dot_general | solution.py:176
  106.0 0.3 copy.25
  106.3 1.0 copy.26
  107.3 0.0 copy-done.1
  107.3 2.1 %fusion.3 = bf16[64,1024]{1,0:T(8,128)(2,1)S(1)} fusion(bf16[1024,64]{1,0:T(8,128)(2,1)S(1)} %bitcast.40, bf16[1024,1792]{1,0:T(8,128)(2,1)} %all-gather.2.cloned.1.call-done), kind=kOutput, calls=%fused_computation.4 | convolution fusion | flops 134283264 | bytes 2359296 | tf_op jit(solution)/shard_map/dot_general | solution.py:176
  109.4 0.7 copy.34
  110.1 0.0 copy-done.2
  110.1 1.3 convolution_convert_fusion.1
  111.4 0.1 copy.28
  111.5 0.8 copy.29
  112.3 0.6 broadcast_in_dim.15.refs_3_
  112.9 23.0 %shard_map.134 = (bf16[4,128,512]{2,1,0:T(8,128)(2,1)}, bf16[4,64,256]{2,1,0:T(8,128)(2,1)}, bf16[4,128,64]{2,1,0:T(8,128)(2,1)}, f32[4,8,256]{2,1,0:T(8,128)}) custom-call(bf16[4,128,512]{2,1,0:T(8,128)(2,1)} %bitcast.33, bf16[4,64,256]{2,1,0:T(8,128)(2,1)} %bitcast.36, bf16[4,128,64]{2,1,0:T(8,128)(2,1)} %bitcast.37, f32[4,8,256]{2,1,0:T(8,128)} %broadcast_in_dim.15.refs_3_), custom_call_target="tpu_custom_call" | custom-call | tf_op jit(solution)/shard_map/pallas_call | solution.py:105
  135.9 1.8 %convert_reduce_fusion = f32[128,512]{1,0:T(8,128)} fusion(bf16[4,128,512]{2,1,0:T(8,128)(2,1)} %get-tuple-element.47), kind=kLoop, calls=%fused_computation.8 | loop fusion | flops 458752 | bytes 786432 | tf_op jit(solution)/shard_map/reduce_sum | solution.py:129
  137.7 1.6 %convert_reduce_fusion.2 = f32[64,256]{1,0:T(8,128)} fusion(bf16[4,64,256]{2,1,0:T(8,128)(2,1)} %get-tuple-element.48), kind=kLoop, calls=%fused_computation.12 | loop fusion | flops 114688 | bytes 196608 | tf_op jit(solution)/shard_map/reduce_sum | solution.py:129
  139.3 0.9 convert_reduce_fusion.1
  140.2 0.7 copy.30
  140.9 0.8 reduce_sum.49
  141.7 0.6 slice.19
  (2 shorter events, 0.1 us)
Async XLA Ops:
  7.2 97.2 %all-gather.2.cloned.1.call-start = ((), (), s32[]{:S(2)}) async-start(), calls=%async_computation | async-start | bytes 4128768 | tf_op jit(solution)/shard_map/all_gather | solution.py:392
  57.0 11.0 %copy-start.3 = (f32[8,8,256]{2,1,0:T(8,128)S(1)}, f32[8,8,256]{2,1,0:T(8,128)}, u32[]{:S(2)}) copy-start(f32[8,8,256]{2,1,0:T(8,128)} %get-tuple-element.46) | copy-start | bytes 196612
  57.0 44.7 %copy-start = (bf16[8,128,128]{2,1,0:T(8,128)(2,1)S(1)}, bf16[8,128,128]{2,1,0:T(8,128)(2,1)}, u32[]{:S(2)}) copy-start(bf16[8,128,128]{2,1,0:T(8,128)(2,1)} %get-tuple-element.39) | copy-start | bytes 786436
  101.7 5.6 %copy-start.1 = (bf16[8,128,64]{2,1,0:T(8,128)(2,1)S(1)}, bf16[8,128,64]{2,1,0:T(8,128)(2,1)}, u32[]{:S(2)}) copy-start(bf16[8,128,64]{2,1,0:T(8,128)(2,1)} %get-tuple-element.44) | copy-start | bytes 393220
  104.3 5.7 %copy-start.2 = (bf16[8,128,128]{2,1,0:T(8,128)(2,1)S(1)}, bf16[8,128,128]{2,1,0:T(8,128)(2,1)}, u32[]{:S(2)}) copy-start(bf16[8,128,128]{2,1,0:T(8,128)(2,1)} %get-tuple-element.45) | copy-start | bytes 786436
Sparse Core Ops, SparseCore 0:
  45.3 51.1 all-gather.1

commit v5 on v3

--- a/solution.py
+++ b/solution.py
@@ -12,6 +12,10 @@
 
 
 NORM_EPS = 1e-05
+
+
+def flipped(index, bit):
+    return index + bit - 2 * bit * lax.rem(index // bit, 2)
 
 
 def exchange_kernel(plan, *refs):
@@ -41,7 +45,16 @@
             device_id_type=pl.DeviceIdType.MESH,
         )
 
-    sent, own, relays, landing = [], [], [], []
+    sent, own, relays, landing, planes = [], [], [], [], []
+
+    def pass_on(block, number, slot, axis, peer):
+        copy = remote(block, block, number, slot, axis, peer)
+        copy.start()
+        sent.append(copy)
+
+    def arrived(block, number, slot, axis, origin):
+        remote(block, block, number, slot, axis, origin).wait_recv()
+
     for number, (kind, axis) in enumerate(plan):
         source, target = sources[number], targets[number]
         size, me = lax.axis_size(axis), lax.axis_index(axis)
@@ -50,6 +63,16 @@
         own[-1].start()
         if kind == "gather":
             sibling = me + 1 - 2 * lax.rem(me, 2)
+            if size == 8:
+                for slot, peer in ((1, flipped(me, 2)), (2, flipped(me, 4))):
+                    copy = remote(source, target.at[me], number, slot, axis, peer)
+                    copy.start()
+                    sent.append(copy)
+                copy = remote(source, target.at[me], number, 0, axis, sibling)
+                copy.start()
+                sent.append(copy)
+                planes.append((number, axis, me, sibling))
+                continue
             for step in range(1, size // 2):
                 copy = remote(
                     source, target.at[me], number, step, axis, lax.rem(me + 2 * step, size)
@@ -76,6 +99,33 @@
                 landing.append(
                     remote(source.at[origin], target.at[origin], number, step, axis, origin)
                 )
+    for number, axis, me, sibling in planes:
+        half = sources[number].shape[0] // 2
+        near, far = flipped(me, 2), flipped(me, 4)
+        for slot, origin, other, start in ((1, near, far, 0), (2, far, near, half)):
+            block = targets[number].at[origin]
+            arrived(block, number, slot, axis, origin)
+            part = targets[number].at[origin, pl.ds(start, half)]
+            pass_on(part, number, 2 + slot, axis, other)
+            pass_on(block, number, 4 + slot, axis, sibling)
+    for number, axis, me, sibling in planes:
+        half = sources[number].shape[0] // 2
+        near, far = flipped(me, 2), flipped(me, 4)
+        across = flipped(near, 4)
+        for slot, origin, start in ((3, far, 0), (4, near, half)):
+            part = targets[number].at[across, pl.ds(start, half)]
+            arrived(part, number, slot, axis, origin)
+            pass_on(part, number, 4 + slot, axis, sibling)
+    for number, axis, me, sibling in planes:
+        half = sources[number].shape[0] // 2
+        near, far = flipped(sibling, 2), flipped(sibling, 4)
+        across = flipped(near, 4)
+        arrived(targets[number].at[sibling], number, 0, axis, sibling)
+        arrived(targets[number].at[near], number, 5, axis, sibling)
+        arrived(targets[number].at[far], number, 6, axis, sibling)
+        for slot, start in ((7, 0), (8, half)):
+            part = targets[number].at[across, pl.ds(start, half)]
+            arrived(part, number, slot, axis, sibling)
     for number, axis, step, origin, sibling in relays:
         size = lax.axis_size(axis)
         block = targets[number].at[origin]
@@ -101,7 +151,7 @@
         )
         for kind, axis, array in items
     ]
-    slots = max(lax.axis_size(axis) for kind, axis in plan)
+    slots = max(lax.axis_size(axis) for kind, axis in plan) + 1
     return pl.pallas_call(
         functools.partial(exchange_kernel, plan),
         out_shape=shapes,
@@ -382,7 +432,7 @@
                 ((rows, features), full),
                 ((rows, features), half),
                 ((rows, middle), half),
-                ((8, middle), full),
+                ((16, middle), full),
                 ((seq_count, rows, width // seq_count), half),
                 ((seq_count, rows, features // seq_count), half),
                 ((rows, width), half),

time: 137 us -> 127 us (0.927)
  Pallas kernels: 123 us -> 113 us
    pallas_call x4, Pallas kernels: 101 us -> 91.3 us  [exchange(): pl.pallas_call(functools.partial(exchange_kernel, plan), out_shape=shapes...]
where the time goes in v5:
time: 127 us; the launch traced here: 126 us
  Pallas kernels  113 us (89%)
  local copies, waits for them, and re-layouts  6.14 us (5%)
  matrix products  3.74 us (3%)
  other arithmetic  2.54 us (2%)
    pallas_call x4, Pallas kernels, exchange(): pl.pallas_call(functools.partial(exchange_kernel, plan), out_shape=shapes...  91.3 us
    pallas_call x3, Pallas kernels, local_call(): pl.pallas_call(kernel, out_shape=[jax.ShapeDtypeStruct(shape, kind) for s...  21.9 us
    dot_general x3, matrix products, nn_dot(): return jnp.dot(left, right, preferred_element_type=jnp.float32)  3.74 us

profile of v5, /device:TPU:0, one launch (start us, length us, event | category | flops | bytes accessed | tf_op | source)
XLA Modules:
  0.0 126.5 jit_solution(8615973854680652106)
XLA Ops:
  0.6 1.4 %copy.27.score_ref = f32[128,1]{1,0:T(8,128)} copy(f32[128,1]{0,1:T(1,128)} %bitcast.48) | data formatting | bytes 1024 | tf_op jit(solution)/shard_map/broadcast_in_dim;squeeze | solution.py:425
  2.0 4.4 %shard_map.128 = (bf16[8,128,128]{2,1,0:T(8,128)(2,1)}, f32[128,2048]{1,0:T(8,128)}, bf16[128,512]{1,0:T(8,128)(2,1)}, bf16[128,1536]{1,0:T(8,128)(2,1)}) custom-call(bf16[128,1024]{1,0:T(8,128)(2,1)} %bitcast.36, bf16[1024,2048]{1,0:T(8,128)(2,1)} %w_in_ref.3), custom_call_target="tpu_custom_call" | custom-call | tf_op jit(solution)/shard_map/pallas_call | solution.py:378
  6.4 23.3 %shard_map.129 = (bf16[8,128,1536]{2,1,0:T(8,128)(2,1)}, bf16[8,128,128]{2,1,0:T(8,128)(2,1)}) custom-call(bf16[128,1536]{1,0:T(8,128)(2,1)} %get-tuple-element.31.refs_0_.own_ref, bf16[8,128,128]{2,1,0:T(8,128)(2,1)} %get-tuple-element.32.refs_1_), custom_call_target="tpu_custom_call" | custom-call | tf_op jit(solution)/shard_map/pallas_call | solution.py:155
  29.7 6.5 %shard_map.130 = (bf16[128,512]{1,0:T(8,128)(2,1)}, f32[128,1024]{1,0:T(8,128)}, bf16[128,1024]{1,0:T(8,128)(2,1)}, bf16[128,256]{1,0:T(8,128)(2,1)}, f32[16,256...) custom-call(s32[1,8]{1,0:T(1,128)} %lengths.3, ...), custom_call_target="tpu_custom_call" | custom-call | tf_op jit(solution)/shard_map/pallas_call | solution.py:378
  36.3 27.4 %shard_map.131 = (bf16[8,128,512]{2,1,0:T(8,128)(2,1)}, bf16[8,128,1024]{2,1,0:T(8,128)(2,1)}, bf16[8,128,256]{2,1,0:T(8,128)(2,1)}, f32[8,16,256]{2,1,0:T(8,128...) custom-call(bf16[128,512]{1,0:T(8,128)(2,1)} %get-tuple-element.36.refs_0_.own_grad_ref, ...), custom_call_target="tpu_custom_call" | custom-call | tf_op jit(solution)/shard_map/pallas_call | solution.py:155
  63.7 0.0 copy-start.6
  63.7 0.0 copy-start.1
  63.7 0.0 copy-start.4
  63.7 0.0 copy-start
  63.7 0.0 copy-start.3
  63.7 11.0 %shard_map.132 = (bf16[128,2048]{1,0:T(8,128)(2,1)}, bf16[128,1024]{1,0:T(8,128)(2,1)}) custom-call(s32[1,8]{1,0:T(1,128)} %lengths.3, s32[1,8]{1,0:T(1,128)} %targets.3, s32[1]{0:T(128)} %bitcast.own_start, bf16[8,128,1536]{2,1,0:T(8,128)(2,1)} %get-tuple-element.33.moved_ref, bf16[8,128,512]{2,1,0:T(8,128)(2,1)} %get-tuple-element.42.grad_all_ref, ...), custom_call_target="tpu_custom_call" | custom-call | tf_op jit(solution)/shard_map/pallas_call | solution.py:378
  74.7 0.0 copy-start.2
  74.7 0.0 copy-done.6
  74.8 0.6 broadcast_in_dim.15.refs_3_
  75.4 0.0 copy-done.1
  75.4 0.0 copy-done.4
  75.4 0.3 fusion.2
  75.7 0.1 copy.31
  75.8 0.8 copy.32
  76.6 0.0 copy-done
  76.6 0.0 copy-done.3
  76.6 0.5 fusion.1
  77.1 0.7 copy.42
  77.8 27.3 %shard_map.133 = (bf16[8,128,2048]{2,1,0:T(8,128)(2,1)}, bf16[4,64,256]{2,1,0:T(8,128)(2,1)}, bf16[4,128,64]{2,1,0:T(8,128)(2,1)}, f32[4,16,256]{2,1,0:T(8,128)}) custom-call(bf16[128,2048]{1,0:T(8,128)(2,1)} %get-tuple-element.47.refs_0_, bf16[4,64,256]{2,1,0:T(8,128)(2,1)} %bitcast.43, bf16[4,128,64]{2,1,0:T(8,128)(2,1)} %bitcast.42, ...), custom_call_target="tpu_custom_call" | custom-call | tf_op jit(solution)/shard_map/pallas_call | solution.py:155
  105.1 0.0 copy-done.2
  105.1 0.0 copy-start.8
  105.1 0.0 copy-start.7
  105.1 0.0 copy-start.5
  105.1 3.0 %fusion = bf16[128,2048]{1,0:T(8,128)(2,1)S(1)} fusion(bf16[8,128,128]{2,1,0:T(8,128)(2,1)S(1)} %copy-done.2, bf16[8,128,2048]{2,1,0:T(8,128)(2,1)} %get-tuple-element.53), kind=kOutput, calls=%fused_computation.1 | convolution fusion | flops 537133056 | bytes 4980736 | tf_op jit(solution)/shard_map/dot_general | solution.py:226
  108.1 0.3 copy.34
  108.4 1.0 copy.35
  109.4 13.3 %shard_map.134 = bf16[4,128,512]{2,1,0:T(8,128)(2,1)} custom-call(bf16[4,128,512]{2,1,0:T(8,128)(2,1)} %bitcast.40), custom_call_target="tpu_custom_call" | custom-call | tf_op jit(solution)/shard_map/pallas_call | solution.py:155
  122.7 1.8 %convert_reduce_fusion = f32[128,512]{1,0:T(8,128)} fusion(bf16[4,128,512]{2,1,0:T(8,128)(2,1)} %shard_map.134), kind=kLoop, calls=%fused_computation.6 | loop fusion | flops 458752 | bytes 786432 | tf_op jit(solution)/shard_map/reduce_sum | solution.py:179
  124.5 0.0 copy-done.8
  124.5 0.6 slice.4
  125.1 0.0 copy-done.7
  125.1 0.6 convert_reduce_fusion.2
  125.7 0.0 copy-done.5
  125.8 0.7 copy.36
  (3 shorter events, 0.1 us)
Async XLA Ops:
  63.7 11.1 %copy-start.6 = (f32[8,16,256]{2,1,0:T(8,128)S(1)}, f32[8,16,256]{2,1,0:T(8,128)}, u32[]{:S(2)}) copy-start(f32[8,16,256]{2,1,0:T(8,128)} %get-tuple-element.52) | copy-start | bytes 393220
  63.7 11.7 %copy-start.1 = (bf16[8,128,256]{2,1,0:T(8,128)(2,1)S(1)}, bf16[8,128,256]{2,1,0:T(8,128)(2,1)}, u32[]{:S(2)}) copy-start(bf16[8,128,256]{2,1,0:T(8,128)(2,1)} %get-tuple-element.51) | copy-start | bytes 1572868
  63.7 11.7 %copy-start.4 = (bf16[8,128,128]{2,1,0:T(8,128)(2,1)S(1)}, bf16[8,128,128]{2,1,0:T(8,128)(2,1)}, u32[]{:S(2)}) copy-start(bf16[8,128,128]{2,1,0:T(8,128)(2,1)} %get-tuple-element.50) | copy-start | bytes 786436
  63.7 12.9 %copy-start = (bf16[8,128,1024]{2,1,0:T(8,128)(2,1)S(1)}, bf16[8,128,1024]{2,1,0:T(8,128)(2,1)}, u32[]{:S(2)}) copy-start(bf16[8,128,1024]{2,1,0:T(8,128)(2,1)} %get-tuple-element.49) | copy-start | bytes 6291460
  63.7 12.8 %copy-start.3 = (bf16[8,128,64]{2,1,0:T(8,128)(2,1)S(1)}, bf16[8,128,64]{2,1,0:T(8,128)(2,1)}, u32[]{:S(2)}) copy-start(bf16[8,128,64]{2,1,0:T(8,128)(2,1)} %get-tuple-element.48) | copy-start | bytes 393220
  74.7 30.3 %copy-start.2 = (bf16[8,128,128]{2,1,0:T(8,128)(2,1)S(1)}, bf16[8,128,128]{2,1,0:T(8,128)(2,1)}, u32[]{:S(2)}) copy-start(bf16[8,128,128]{2,1,0:T(8,128)(2,1)} %get-tuple-element.46) | copy-start | bytes 786436
  105.1 19.4 %copy-start.8 = (f32[4,16,256]{2,1,0:T(8,128)S(1)}, f32[4,16,256]{2,1,0:T(8,128)}, u32[]{:S(2)}) copy-start(f32[4,16,256]{2,1,0:T(8,128)} %get-tuple-element.56) | copy-start | bytes 196612
  105.1 20.0 %copy-start.7 = (bf16[4,64,256]{2,1,0:T(8,128)(2,1)S(1)}, bf16[4,64,256]{2,1,0:T(8,128)(2,1)}, u32[]{:S(2)}) copy-start(bf16[4,64,256]{2,1,0:T(8,128)(2,1)} %get-tuple-element.54) | copy-start | bytes 393220
  105.1 20.6 %copy-start.5 = (bf16[4,128,64]{2,1,0:T(8,128)(2,1)S(1)}, bf16[4,128,64]{2,1,0:T(8,128)(2,1)}, u32[]{:S(2)}) copy-start(bf16[4,128,64]{2,1,0:T(8,128)(2,1)} %get-tuple-element.55) | copy-start | bytes 196612

commit v6 on v5

--- a/solution.py
+++ b/solution.py
@@ -299,7 +299,11 @@
     out_b = output.astype(jnp.bfloat16)
     store_blocks(out_ref, out_b)
     mid_act = nn_dot(out_b, w_score_ref[...])
-    weight_c = score_ref[...] * query_tgt.astype(jnp.float32)
+    diagonal = lax.broadcasted_iota(jnp.int32, (rows, rows), 0) == lax.broadcasted_iota(
+        jnp.int32, (rows, rows), 1
+    )
+    score_col = jnp.sum(jnp.where(diagonal, score_ref[...], 0.0), axis=1, keepdims=True)
+    weight_c = score_col * query_tgt.astype(jnp.float32)
     head_part = jnp.sum(weight_c * jax.nn.silu(mid_act), axis=0, keepdims=True)
     head_ref[...] = jnp.broadcast_to(head_part, head_ref.shape)
     d_mid_b = (weight_c * head_score_ref[...] * silu_slope(mid_act)).astype(jnp.bfloat16)
@@ -422,7 +426,7 @@
                 pre_act,
                 x_rows[0],
                 grad_out[0],
-                grad_score[0][:, None],
+                grad_score,
                 head_score[None, :],
                 w_out,
                 w_score,

time: 127 us -> 125 us (0.984)
  local copies, waits for them, and re-layouts: 6.14 us -> 4.75 us
    another operation x1 -> x0, local copies, waits for them, and re-layouts: 1.39 us -> none  [on_device(): grad_score[0][:, None]]
where the time goes in v6:
time: 125 us
  Pallas kernels  113 us (90%)
  local copies, waits for them, and re-layouts  4.75 us (4%)
  matrix products  3.74 us (3%)
  other arithmetic  2.54 us (2%)
    pallas_call x4, Pallas kernels, exchange(): pl.pallas_call(functools.partial(exchange_kernel, plan), out_shape=shapes...  91.3 us
    pallas_call x3, Pallas kernels, local_call(): pl.pallas_call(kernel, out_shape=[jax.ShapeDtypeStruct(shape, kind) for s...  21.9 us
    dot_general x3, matrix products, nn_dot(): return jnp.dot(left, right, preferred_element_type=jnp.float32)  3.74 us
    reduce_sum x4, other arithmetic, group_sum(): return jnp.sum(array.astype(jnp.float32), axis=0)  2.52 us

profile of v6, /device:TPU:0, one launch (start us, length us, event | category | flops | bytes accessed | tf_op | source)
XLA Modules:
  0.0 125.0 jit_solution(5022475590622137731)
XLA Ops:
  0.6 4.4 %shard_map.128 = (bf16[8,128,128]{2,1,0:T(8,128)(2,1)}, f32[128,2048]{1,0:T(8,128)}, bf16[128,512]{1,0:T(8,128)(2,1)}, bf16[128,1536]{1,0:T(8,128)(2,1)}) custom-call(bf16[128,1024]{1,0:T(8,128)(2,1)} %bitcast.35, bf16[1024,2048]{1,0:T(8,128)(2,1)} %w_in_ref.3), custom_call_target="tpu_custom_call" | custom-call | tf_op jit(solution)/shard_map/pallas_call | solution.py:382
  5.0 23.3 %shard_map.129 = (bf16[8,128,1536]{2,1,0:T(8,128)(2,1)}, bf16[8,128,128]{2,1,0:T(8,128)(2,1)}) custom-call(bf16[128,1536]{1,0:T(8,128)(2,1)} %get-tuple-element.31.refs_0_.own_ref, bf16[8,128,128]{2,1,0:T(8,128)(2,1)} %get-tuple-element.32.refs_1_), custom_call_target="tpu_custom_call" | custom-call | tf_op jit(solution)/shard_map/pallas_call | solution.py:155
  28.3 6.5 %shard_map.130 = (bf16[128,512]{1,0:T(8,128)(2,1)}, f32[128,1024]{1,0:T(8,128)}, bf16[128,1024]{1,0:T(8,128)(2,1)}, bf16[128,256]{1,0:T(8,128)(2,1)}, f32[16,256...) custom-call(s32[1,8]{1,0:T(1,128)} %lengths.3, ...), custom_call_target="tpu_custom_call" | custom-call | tf_op jit(solution)/shard_map/pallas_call | solution.py:382
  34.8 27.4 %shard_map.131 = (bf16[8,128,512]{2,1,0:T(8,128)(2,1)}, bf16[8,128,1024]{2,1,0:T(8,128)(2,1)}, bf16[8,128,256]{2,1,0:T(8,128)(2,1)}, f32[8,16,256]{2,1,0:T(8,128...) custom-call(bf16[128,512]{1,0:T(8,128)(2,1)} %get-tuple-element.36.refs_0_.own_grad_ref, ...), custom_call_target="tpu_custom_call" | custom-call | tf_op jit(solution)/shard_map/pallas_call | solution.py:155
  62.2 0.0 copy-start.6
  62.3 0.0 copy-start.1
  62.3 0.0 copy-start.4
  62.3 0.0 copy-start
  62.3 0.0 copy-start.3
  62.3 11.0 %shard_map.132 = (bf16[128,2048]{1,0:T(8,128)(2,1)}, bf16[128,1024]{1,0:T(8,128)(2,1)}) custom-call(s32[1,8]{1,0:T(1,128)} %lengths.3, s32[1,8]{1,0:T(1,128)} %targets.3, s32[1]{0:T(128)} %bitcast.own_start, bf16[8,128,1536]{2,1,0:T(8,128)(2,1)} %get-tuple-element.33.moved_ref, bf16[8,128,512]{2,1,0:T(8,128)(2,1)} %get-tuple-element.42.grad_all_ref, ...), custom_call_target="tpu_custom_call" | custom-call | tf_op jit(solution)/shard_map/pallas_call | solution.py:382
  73.3 0.0 copy-start.2
  73.3 0.0 copy-done.6
  73.3 0.6 broadcast_in_dim.15.refs_3_
  74.0 0.0 copy-done.1
  74.0 0.0 copy-done.4
  74.0 0.3 fusion.2
  74.2 0.1 copy.28
  74.4 0.8 copy.29
  75.1 0.0 copy-done
  75.1 0.0 copy-done.3
  75.1 0.5 fusion.1
  75.6 0.7 copy.39
  76.3 27.3 %shard_map.133 = (bf16[8,128,2048]{2,1,0:T(8,128)(2,1)}, bf16[4,64,256]{2,1,0:T(8,128)(2,1)}, bf16[4,128,64]{2,1,0:T(8,128)(2,1)}, f32[4,16,256]{2,1,0:T(8,128)}) custom-call(bf16[128,2048]{1,0:T(8,128)(2,1)} %get-tuple-element.47.refs_0_, bf16[4,64,256]{2,1,0:T(8,128)(2,1)} %bitcast.42, bf16[4,128,64]{2,1,0:T(8,128)(2,1)} %bitcast.41, ...), custom_call_target="tpu_custom_call" | custom-call | tf_op jit(solution)/shard_map/pallas_call | solution.py:155
  103.6 0.0 copy-done.2
  103.6 0.0 copy-start.8
  103.7 0.0 copy-start.7
  103.7 0.0 copy-start.5
  103.7 3.0 %fusion = bf16[128,2048]{1,0:T(8,128)(2,1)S(1)} fusion(bf16[8,128,128]{2,1,0:T(8,128)(2,1)S(1)} %copy-done.2, bf16[8,128,2048]{2,1,0:T(8,128)(2,1)} %get-tuple-element.53), kind=kOutput, calls=%fused_computation.1 | convolution fusion | flops 537133056 | bytes 4980736 | tf_op jit(solution)/shard_map/dot_general | solution.py:226
  106.7 0.3 copy.31
  106.9 1.0 copy.32
  107.9 13.3 %shard_map.134 = bf16[4,128,512]{2,1,0:T(8,128)(2,1)} custom-call(bf16[4,128,512]{2,1,0:T(8,128)(2,1)} %bitcast.39), custom_call_target="tpu_custom_call" | custom-call | tf_op jit(solution)/shard_map/pallas_call | solution.py:155
  121.2 1.8 %convert_reduce_fusion = f32[128,512]{1,0:T(8,128)} fusion(bf16[4,128,512]{2,1,0:T(8,128)(2,1)} %shard_map.134), kind=kLoop, calls=%fused_computation.6 | loop fusion | flops 458752 | bytes 786432 | tf_op jit(solution)/shard_map/reduce_sum | solution.py:179
  123.1 0.0 copy-done.8
  123.1 0.6 slice.4
  123.6 0.0 copy-done.7
  123.6 0.6 convert_reduce_fusion.2
  124.3 0.0 copy-done.5
  124.3 0.7 copy.33
  (3 shorter events, 0.1 us)
Async XLA Ops:
  62.2 11.1 %copy-start.6 = (f32[8,16,256]{2,1,0:T(8,128)S(1)}, f32[8,16,256]{2,1,0:T(8,128)}, u32[]{:S(2)}) copy-start(f32[8,16,256]{2,1,0:T(8,128)} %get-tuple-element.52) | copy-start | bytes 393220
  62.3 11.7 %copy-start.1 = (bf16[8,128,256]{2,1,0:T(8,128)(2,1)S(1)}, bf16[8,128,256]{2,1,0:T(8,128)(2,1)}, u32[]{:S(2)}) copy-start(bf16[8,128,256]{2,1,0:T(8,128)(2,1)} %get-tuple-element.51) | copy-start | bytes 1572868
  62.3 11.7 %copy-start.4 = (bf16[8,128,128]{2,1,0:T(8,128)(2,1)S(1)}, bf16[8,128,128]{2,1,0:T(8,128)(2,1)}, u32[]{:S(2)}) copy-start(bf16[8,128,128]{2,1,0:T(8,128)(2,1)} %get-tuple-element.50) | copy-start | bytes 786436
  62.3 12.9 %copy-start = (bf16[8,128,1024]{2,1,0:T(8,128)(2,1)S(1)}, bf16[8,128,1024]{2,1,0:T(8,128)(2,1)}, u32[]{:S(2)}) copy-start(bf16[8,128,1024]{2,1,0:T(8,128)(2,1)} %get-tuple-element.49) | copy-start | bytes 6291460
  62.3 12.9 %copy-start.3 = (bf16[8,128,64]{2,1,0:T(8,128)(2,1)S(1)}, bf16[8,128,64]{2,1,0:T(8,128)(2,1)}, u32[]{:S(2)}) copy-start(bf16[8,128,64]{2,1,0:T(8,128)(2,1)} %get-tuple-element.48) | copy-start | bytes 393220
  73.3 30.3 %copy-start.2 = (bf16[8,128,128]{2,1,0:T(8,128)(2,1)S(1)}, bf16[8,128,128]{2,1,0:T(8,128)(2,1)}, u32[]{:S(2)}) copy-start(bf16[8,128,128]{2,1,0:T(8,128)(2,1)} %get-tuple-element.46) | copy-start | bytes 786436
  103.6 19.4 %copy-start.8 = (f32[4,16,256]{2,1,0:T(8,128)S(1)}, f32[4,16,256]{2,1,0:T(8,128)}, u32[]{:S(2)}) copy-start(f32[4,16,256]{2,1,0:T(8,128)} %get-tuple-element.56) | copy-start | bytes 196612
  103.7 20.0 %copy-start.7 = (bf16[4,64,256]{2,1,0:T(8,128)(2,1)S(1)}, bf16[4,64,256]{2,1,0:T(8,128)(2,1)}, u32[]{:S(2)}) copy-start(bf16[4,64,256]{2,1,0:T(8,128)(2,1)} %get-tuple-element.54) | copy-start | bytes 393220
  103.7 20.6 %copy-start.5 = (bf16[4,128,64]{2,1,0:T(8,128)(2,1)S(1)}, bf16[4,128,64]{2,1,0:T(8,128)(2,1)}, u32[]{:S(2)}) copy-start(bf16[4,128,64]{2,1,0:T(8,128)(2,1)} %get-tuple-element.55) | copy-start | bytes 196612
